TPU v7x, 256 devices: a whole 4x4x8 slice. The times are simulated.
256 devices in a mesh: ctx: 64 (over x, z, y_lo), head: 4 (over y_hi, core).
Axes of the slice: x: 4, y: 4 (y_hi: 2, y_lo: 2; y = y_hi * 2 + y_lo), z: 8, core: 2. Of those that a mesh axis runs over, the one named last changes fastest.
Arguments:
- queries: bfloat16 [24576, 8192], P('ctx', 'head'), may hold values from -160 to 160
- keys: bfloat16 [24576, 1024], P('ctx', 'head'), may hold values from -4 to 4
- values: bfloat16 [24576, 1024], P('ctx', 'head'), may hold values from -6 to 6
- keep_rows: int32 [64, 8, 64, 4], P('ctx', 'head'), may hold values from 0 to 383
- keep_dest: int32 [64, 8, 64], P('ctx', 'head'), may hold values from 0 to 63, as said below
- keep_count: int32 [64, 8, 64], P('ctx', 'head'), may hold values from 1 to 4, as said below
Outputs:
- attended: bfloat16 [24576, 8192], P('ctx', 'head')
- key_scores: float32 [24576], P('ctx')
- decode_cache: bfloat16 [64, 64, 4, 8, 256], P('ctx', None, None, 'head')
Inputs may be any that keep to these rules, and one draw needn't show every extreme that they name: For each source shard and head, keep_dest over j is a permutation of 0 to 63. `keep_count`: in every draw some decode shard receives 4 live slots in every block.
All inputs are finite; a program needn't handle non-finite values.
Results may differ from a plain program's by a relative error of at most 0.0045.
Values may be sent and summed in bfloat16 or wider, within the bound.
A program may use at most 64 MiB of HBM per device.

v0:
```python
import jax
import jax.numpy as jnp
from jax import lax
from jax.sharding import PartitionSpec as P

HD = 128
KB = 4
QH = 64


def passed_along(block, axis, distance):
    devices = range(lax.axis_size(axis))
    route = [((i - distance) % len(devices), i) for i in devices]
    return lax.ppermute(block, axis, route)


def block_positions(shard, count, half):
    index = jnp.arange(2 * half, dtype=jnp.int32)
    return jnp.where(
        index < half, shard * half + index, (2 * count - 1 - shard) * half + index - half
    )


def on_device(queries, keys, values, keep_rows, keep_dest, keep_count):
    count = lax.axis_size("ctx")
    shard = lax.axis_index("ctx")
    tok = keys.shape[0]
    half = tok // 2
    groups = keys.shape[1] // HD
    scale = HD ** (-0.5)
    pair = jnp.concatenate([keys.reshape(tok, groups, HD), values.reshape(tok, groups, HD)], axis=2)
    block_index = jnp.arange(count, dtype=jnp.int32)
    slot = jnp.arange(KB, dtype=jnp.int32)
    outgoing = []
    for group in range(groups):
        rows_g = keep_rows[0, group]
        live_g = keep_count[0, group]
        dest_g = keep_dest[0, group]
        picked = jnp.take(pair[:, group], rows_g.reshape(-1), axis=0).reshape(count, KB, 2 * HD)
        picked = jnp.where(
            (slot[None, :] < live_g[:, None])[..., None], picked, jnp.zeros((), jnp.bfloat16)
        )
        match = dest_g[:, None] == block_index[None, :]
        inverse = jnp.sum(block_index[:, None] * match, axis=0)
        outgoing.append(jnp.take(picked, inverse, axis=0))
    outgoing = jnp.stack(outgoing, axis=2)[None]
    decode_cache = lax.all_to_all(outgoing, "ctx", split_axis=1, concat_axis=1, tiled=True)
    blocks = [pair]
    for step in range(2):
        blocks.append(passed_along(blocks[-1], "ctx", 1))
    kv_all = jnp.concatenate(blocks, 0)
    key_pos = jnp.concatenate(
        [block_positions((shard - step) % count, count, half) for step in range(3)]
    )
    query_pos = block_positions(shard, count, half)
    query_view = queries.reshape(tok, groups, -1, HD)
    column = jnp.zeros((3 * tok,), jnp.float32)
    results = []
    for group in range(groups):
        key_g = kv_all[:, group, :HD]
        val_g = kv_all[:, group, HD:]
        pieces = []
        for part_half in range(2):
            query_g = query_view[part_half * half : (part_half + 1) * half, group]
            score = (
                jnp.einsum("qrd,kd->rqk", query_g, key_g, preferred_element_type=jnp.float32)
                * scale
            )
            allowed = key_pos[None, :] <= query_pos[part_half * half : (part_half + 1) * half, None]
            score = jnp.where(allowed[None], score, -jnp.inf)
            top = jnp.max(score, -1, keepdims=True)
            weight = jnp.exp(score - top)
            total = jnp.sum(weight, -1, keepdims=True)
            product = jnp.einsum(
                "rqk,kd->qrd",
                weight.astype(jnp.bfloat16),
                val_g,
                preferred_element_type=jnp.float32,
            )
            pieces.append(product / jnp.transpose(total, (1, 0, 2)))
            column = column + jnp.sum(weight / total, axis=(0, 1))
        results.append(jnp.concatenate(pieces, 0))
    attended = jnp.stack(results, 1).reshape(tok, -1).astype(jnp.bfloat16)
    terms = column.reshape(3, tok) / QH
    carry = terms[2]
    for step in range(2):
        carry = passed_along(carry, "ctx", -1) + terms[1 - step]
    carry = lax.psum(carry, "head")
    return (attended, carry, decode_cache)


def solution(mesh):
    return jax.shard_map(
        on_device,
        mesh=mesh,
        in_specs=(
            P("ctx", "head"),
            P("ctx", "head"),
            P("ctx", "head"),
            P("ctx", "head", None, None),
            P("ctx", "head", None),
            P("ctx", "head", None),
        ),
        out_specs=(P("ctx", "head"), P("ctx"), P("ctx", None, None, "head", None)),
        check_vma=False,
    )
```

profile of v0, /device:TPU:1, one launch (start us, length us, event | category | flops | bytes accessed | tf_op | source)
XLA Modules:
  0.0 109.0 jit_solution(9795593275014475528)
XLA Ops:
  0.6 0.8 slice_bitcast_fusion.22
  1.5 0.7 fusion.76
  2.7 0.8 slice_bitcast_fusion.23
  3.5 1.1 %copy.56 = bf16[384,256]{0,1:T(8,128)(2,1)S(1)} copy(bf16[384,256]{1,0:T(8,128)(2,1)} %param.11) | data formatting | bytes 393216 | tf_op args[1]
  4.8 1.1 %copy.57 = bf16[384,256]{0,1:T(8,128)(2,1)S(1)} copy(bf16[384,256]{1,0:T(8,128)(2,1)} %param.12) | data formatting | bytes 393216 | tf_op args[2]
  6.1 1.2 %gather_fusion = bf16[256,256]{1,0:T(8,128)(2,1)S(1)} fusion(bf16[384,256]{1,0:T(8,128)(2,1)S(1)} %get-tuple-element.21, s32[1024]{0:T(1024)S(1)} %pad_clamp_fusion.3), kind=kCustom, calls=%fused_computation.clone | custom fusion | bytes 263168 | tf_op jit(solution)/shard_map/jit(_take)/gather | solution.py:39
  8.5 1.2 %gather_fusion.2 = bf16[256,256]{1,0:T(8,128)(2,1)S(1)} fusion(bf16[384,256]{1,0:T(8,128)(2,1)S(1)} %get-tuple-element.22, s32[1024]{0:T(1024)S(1)} %pad_clamp_fusion.1), kind=kCustom, calls=%fused_computation.2.clone | custom fusion | bytes 263168 | tf_op jit(solution)/shard_map/jit(_take)/gather | solution.py:39
  10.9 1.0 copy.70
  11.9 13.5 %all-to-all-start = ((bf16[1,64,4,2,256]{4,3,2,0,1:T(2,128)(2,1)}), bf16[1,64,4,2,256]{4,3,2,0,1:T(2,128)(2,1)S(1)}, u32[]{:S(2)}, u32[]{:S(2)}) async-start(bf16[1,64,4,2,256]{4,3,2,0,1:T(2,128)(2,1)} %copy.70), calls=%async_computation | async-start | bytes 524288 | tf_op jit(solution)/shard_map/all_to_all | solution.py:47
  25.4 1.1 collective-permute-start
  26.6 1.9 %copy.60 = bf16[384,2048]{0,1:T(8,128)(2,1)S(1)} copy(bf16[384,2048]{1,0:T(8,128)(2,1)} %param.10) | data formatting | bytes 3145728 | tf_op args[0]
  28.5 16.5 %collective-permute-done = bf16[384,2,256]{2,0,1:T(8,128)(2,1)S(1)} collective-permute-done((bf16[384,2,256]{2,0,1:T(8,128)(2,1)S(1)}, bf16[384,2,256]{2,0,1:T(8,128)(2,1)S(1)}, u32[]{:S(2)}, u32[]{:S(2)}) %collective-permute-start) | collective-permute-done | bytes 393248 | tf_op jit(solution)/shard_map/ppermute | solution.py:14
  45.3 13.0 %collective-permute-done.1 = bf16[384,2,256]{2,0,1:T(8,128)(2,1)S(1)} collective-permute-done((bf16[384,2,256]{2,0,1:T(8,128)(2,1)S(1)}, bf16[384,2,256]{2,0,1:T(8,128)(2,1)S(1)}, u32[]{:S(2)}, u32[]{:S(2)}) %collective-permute-start.1) | collective-permute-done | bytes 393248 | tf_op jit(solution)/shard_map/ppermute | solution.py:14
  58.4 1.9 %fusion.1 = (f32[8,192]{1,0:T(8,128)S(1)}, f32[1152,192,8]{0,1,2:T(8,128)S(1)}) fusion(pred[192,1152]{1,0:T(8,128)(4,1)S(1)} %get-tuple-element.24, bf16[384,2,8,128]{0,3,2,1:T(8,128)(2,1)S(1)} %bitcast.206, bf16[1152,2,256]{2,0,1:T(8,128)(2,1)S(1)} %pad_maximum_fusion.1), kind=kOutput, calls=%fused_computation.17 | convolution fusion | flops 458291712 | bytes 8124416 | tf_op jit(solution)/shard_map/qrd,kd->rqk/dot_general | solution.py:66
  60.3 2.1 %fusion.6 = f32[8,192]{1,0:T(8,128)S(1)} fusion(f32[1152,192,8]{0,1,2:T(8,128)S(1)} %get-tuple-element.34, f32[8,192]{1,0:T(8,128)S(1)} %get-tuple-element.33, pred[192,1152]{1,0:T(8,128)(4,1)S(1)} %get-tuple-element.24), kind=kLoop, calls=%fused_computation.22 | loop fusion | flops 7076352 | bytes 7311360 | tf_op jit(solution)/shard_map/reduce_sum | solution.py:73
  62.4 3.6 %divide_reduce_fusion.2 = (f32[1152]{0:T(1024)S(1)}, f32[8,192]{1,0:T(8,128)S(1)}, f32[1152,192,8]{0,1,2:T(8,128)S(1)}) fusion(f32[1152,192,8]{0,1,2:T(8,128)S(1)} %get-tuple-element.34, f32[8,192]{1,0:T(8,128)S(1)} %fusion.6, f32[8,192]{1,0:T(8,128)S(1)} %get-tuple-element.33, pred[192,1152]{1,0:T(8,128)(4,1)S(1)} %get-tuple-element.24, ...), kind=kOutput, calls=%fused_computation.14 | convolution fusion | flops 467137920 | bytes 15223296 | tf_op jit(solution)/shard_map/qrd,kd->rqk/dot_general | solution.py:66
  66.0 1.9 %fusion.51 = bf16[192,8,128]{2,0,1:T(8,128)(2,1)S(1)} fusion(f32[1152,192,8]{0,1,2:T(8,128)S(1)} %get-tuple-element.34, f32[8,192]{1,0:T(8,128)S(1)} %get-tuple-element.33, pred[192,1152]{1,0:T(8,128)(4,1)S(1)} %get-tuple-element.24, f32[192,8]{0,1:T(8,128)S(1)} %bitcast.218, bf16[1152,2,256]{2,0,1:T(8,128)(2,1)S(1)} %pad_maximum_fusion.1), kind=kOutput, calls=%fused_computation.47 | convolution fusion | flops 460455936 | bytes 8003584 | tf_op jit(solution)/shard_map/rqk,kd->qrd/dot_general | solution.py:74
  67.9 1.9 %fusion.10 = f32[8,192]{1,0:T(8,128)S(1)} fusion(f32[1152,192,8]{0,1,2:T(8,128)S(1)} %get-tuple-element.35, f32[8,192]{1,0:T(8,128)S(1)} %get-tuple-element.18, pred[192,1152]{1,0:T(8,128)(4,1)S(1)} %get-tuple-element.24), kind=kLoop, calls=%fused_computation.26 | loop fusion | flops 7076352 | bytes 7311360 | tf_op jit(solution)/shard_map/reduce_sum | solution.py:73
  69.8 1.8 %divide_reduce_fusion = f32[1152]{0:T(1024)S(1)} fusion(f32[1152,192,8]{0,1,2:T(8,128)S(1)} %get-tuple-element.35, f32[8,192]{1,0:T(8,128)S(1)} %fusion.10, f32[8,192]{1,0:T(8,128)S(1)} %get-tuple-element.18, pred[192,1152]{1,0:T(8,128)(4,1)S(1)} %get-tuple-element.24), kind=kLoop, calls=%fused_computation.12 | loop fusion | flops 8846208 | bytes 7315968 | tf_op jit(solution)/shard_map/reduce_sum | solution.py:81
  71.6 1.9 %fusion.39 = bf16[192,8,128]{2,0,1:T(8,128)(2,1)S(1)} fusion(f32[1152,192,8]{0,1,2:T(8,128)S(1)} %get-tuple-element.35, f32[8,192]{1,0:T(8,128)S(1)} %get-tuple-element.18, pred[192,1152]{1,0:T(8,128)(4,1)S(1)} %get-tuple-element.24, f32[192,8]{0,1:T(8,128)S(1)} %bitcast.216, bf16[1152,2,256]{2,0,1:T(8,128)(2,1)S(1)} %pad_maximum_fusion.1), kind=kOutput, calls=%fused_computation.43 | convolution fusion | flops 460455936 | bytes 8003584 | tf_op jit(solution)/shard_map/rqk,kd->qrd/dot_general | solution.py:74
  73.5 1.7 %fusion = (f32[8,192]{1,0:T(8,128)S(1)}, f32[1152,192,8]{0,1,2:T(8,128)S(1)}) fusion(pred[192,1152]{1,0:T(8,128)(4,1)S(1)} %get-tuple-element.23, bf16[384,2,8,128]{0,3,2,1:T(8,128)(2,1)S(1)} %bitcast.208, bf16[1152,2,256]{2,0,1:T(8,128)(2,1)S(1)} %pad_maximum_fusion.1), kind=kOutput, calls=%fused_computation.16 | convolution fusion | flops 458291712 | bytes 8124416 | tf_op jit(solution)/shard_map/qrd,kd->rqk/dot_general | solution.py:66
  75.2 2.1 %fusion.4 = f32[8,192]{1,0:T(8,128)S(1)} fusion(f32[1152,192,8]{0,1,2:T(8,128)S(1)} %get-tuple-element.37, f32[8,192]{1,0:T(8,128)S(1)} %get-tuple-element.36, pred[192,1152]{1,0:T(8,128)(4,1)S(1)} %get-tuple-element.23), kind=kLoop, calls=%fused_computation.20 | loop fusion | flops 7076352 | bytes 7311360 | tf_op jit(solution)/shard_map/reduce_sum | solution.py:73
  77.3 3.4 %divide_reduce_fusion.3 = (f32[1152]{0:T(1024)S(1)}, f32[8,192]{1,0:T(8,128)S(1)}, f32[1152,192,8]{0,1,2:T(8,128)S(1)}) fusion(f32[1152,192,8]{0,1,2:T(8,128)S(1)} %get-tuple-element.37, f32[8,192]{1,0:T(8,128)S(1)} %fusion.4, f32[8,192]{1,0:T(8,128)S(1)} %get-tuple-element.36, pred[192,1152]{1,0:T(8,128)(4,1)S(1)} %get-tuple-element.23, ...), kind=kOutput, calls=%fused_computation.15 | convolution fusion | flops 467137920 | bytes 15223296 | tf_op jit(solution)/shard_map/qrd,kd->rqk/dot_general | solution.py:66
  80.7 1.9 %fusion.57 = bf16[192,8,128]{2,0,1:T(8,128)(2,1)S(1)} fusion(f32[1152,192,8]{0,1,2:T(8,128)S(1)} %get-tuple-element.37, f32[8,192]{1,0:T(8,128)S(1)} %get-tuple-element.36, pred[192,1152]{1,0:T(8,128)(4,1)S(1)} %get-tuple-element.23, f32[192,8]{0,1:T(8,128)S(1)} %bitcast.217, bf16[1152,2,256]{2,0,1:T(8,128)(2,1)S(1)} %pad_maximum_fusion.1), kind=kOutput, calls=%fused_computation.49 | convolution fusion | flops 460455936 | bytes 8003584 | tf_op jit(solution)/shard_map/rqk,kd->qrd/dot_general | solution.py:74
  82.6 1.9 %fusion.8 = f32[8,192]{1,0:T(8,128)S(1)} fusion(f32[1152,192,8]{0,1,2:T(8,128)S(1)} %get-tuple-element.38, f32[8,192]{1,0:T(8,128)S(1)} %get-tuple-element.20, pred[192,1152]{1,0:T(8,128)(4,1)S(1)} %get-tuple-element.23), kind=kLoop, calls=%fused_computation.24 | loop fusion | flops 7076352 | bytes 7311360 | tf_op jit(solution)/shard_map/reduce_sum | solution.py:73
  84.5 1.8 %divide_reduce_fusion.1 = f32[1152]{0:T(1024)S(1)} fusion(f32[1152,192,8]{0,1,2:T(8,128)S(1)} %get-tuple-element.38, f32[8,192]{1,0:T(8,128)S(1)} %fusion.8, f32[8,192]{1,0:T(8,128)S(1)} %get-tuple-element.20, pred[192,1152]{1,0:T(8,128)(4,1)S(1)} %get-tuple-element.23), kind=kLoop, calls=%fused_computation.13 | loop fusion | flops 8846208 | bytes 7315968 | tf_op jit(solution)/shard_map/reduce_sum | solution.py:81
  86.3 1.9 %fusion.45 = bf16[192,8,128]{2,0,1:T(8,128)(2,1)S(1)} fusion(f32[1152,192,8]{0,1,2:T(8,128)S(1)} %get-tuple-element.38, f32[8,192]{1,0:T(8,128)S(1)} %get-tuple-element.20, pred[192,1152]{1,0:T(8,128)(4,1)S(1)} %get-tuple-element.23, f32[192,8]{0,1:T(8,128)S(1)} %bitcast.215, bf16[1152,2,256]{2,0,1:T(8,128)(2,1)S(1)} %pad_maximum_fusion.1), kind=kOutput, calls=%fused_computation.45 | convolution fusion | flops 460455936 | bytes 8003584 | tf_op jit(solution)/shard_map/rqk,kd->qrd/dot_general | solution.py:74
  88.5 2.3 %collective-permute-done.2 = f32[384]{0:T(512)S(1)} collective-permute-done((f32[384]{0:T(512)S(1)}, f32[384]{0:T(512)S(1)}, u32[]{:S(2)}, u32[]{:S(2)}) %collective-permute-start.2) | collective-permute-done | bytes 1568 | tf_op jit(solution)/shard_map/ppermute | solution.py:14
  90.8 4.2 %collective-permute-start.3 = (f32[384]{0:T(512)S(1)}, f32[384]{0:T(512)S(1)}, u32[]{:S(2)}, u32[]{:S(2)}) collective-permute-start(f32[384]{0:T(512)S(1)} %slice_add_fusion.1), channel_id=1, source_target_pairs={{4,0},{8,4},{12,8},{16,12},{20,16},{24,20},{28,24},{32,28},{36,32}... | collective-permute-start | bytes 4616 | tf_op jit(solution)/shard_map/ppermute | solution.py:14
  95.2 0.9 copy.65
  96.0 1.6 %copy.71 = bf16[384,2048]{1,0:T(8,128)(2,1)} copy(bf16[384,2048]{0,1:T(8,128)(2,1)S(1)} %bitcast.205) | data formatting | bytes 3145728
  97.7 10.6 %psum.7 = f32[384]{0:T(512)} all-reduce(f32[384]{0:T(512)S(1)} %slice_add_fusion), channel_id=1, replica_groups=mesh['ctx'=64,'head'=4] {'head'}, use_global_device_ids=true, to_apply=%region_12.13 | all-reduce | flops 384 | bytes 3072 | tf_op jit(solution)/shard_map/psum | solution.py:88
  (58 shorter events, 5.0 us)
Async XLA Ops:
  11.9 33.4 %all-to-all-start = ((bf16[1,64,4,2,256]{4,3,2,0,1:T(2,128)(2,1)}), bf16[1,64,4,2,256]{4,3,2,0,1:T(2,128)(2,1)S(1)}, u32[]{:S(2)}, u32[]{:S(2)}) async-start(bf16[1,64,4,2,256]{4,3,2,0,1:T(2,128)(2,1)} %copy.70), calls=%async_computation | async-start | bytes 524288 | tf_op jit(solution)/shard_map/all_to_all | solution.py:47
  25.4 19.5 %collective-permute-start = (bf16[384,2,256]{2,0,1:T(8,128)(2,1)S(1)}, bf16[384,2,256]{2,0,1:T(8,128)(2,1)S(1)}, u32[]{:S(2)}, u32[]{:S(2)}) collective-permute-start(bf16[384,2,256]{2,0,1:T(8,128)(2,1)S(1)} %pad_maximum_fusion.2), channel_id=1, source_target_pairs={{252,0},{0,4},{4,8},{8,12},{12,16},{16,20},{20,24},{24,28},{28,32}... | collective-permute-start | bytes 1179656 | tf_op jit(solution)/shard_map/ppermute | solution.py:14
  45.0 13.4 %collective-permute-start.1 = (bf16[384,2,256]{2,0,1:T(8,128)(2,1)S(1)}, bf16[384,2,256]{2,0,1:T(8,128)(2,1)S(1)}, u32[]{:S(2)}, u32[]{:S(2)}) collective-permute-start(bf16[384,2,256]{2,0,1:T(8,128)(2,1)S(1)} %collective-permute-done), channel_id=1, source_target_pairs={{252,0},{0,4},{4,8},{8,12},{12,16},{16,20},{20,24},{24,28},{28,32}... | collective-permute-start | bytes 1179656 | tf_op jit(solution)/shard_map/ppermute | solution.py:14
  45.3 17.1 %copy-start = (bf16[1,64,4,2,256]{4,3,2,0,1:T(2,128)(2,1)}, bf16[1,64,4,2,256]{4,3,2,0,1:T(2,128)(2,1)S(1)}, u32[]{:S(2)}) copy-start(bf16[1,64,4,2,256]{4,3,2,0,1:T(2,128)(2,1)S(1)} %all-to-all-done) | copy-start | bytes 786436
  88.2 20.1 %copy-start.1 = (bf16[1,64,4,2,256]{4,3,2,0,1:T(2,128)(2,1)S(1)}, bf16[1,64,4,2,256]{4,3,2,0,1:T(2,128)(2,1)}, u32[]{:S(2)}) copy-start(bf16[1,64,4,2,256]{4,3,2,0,1:T(2,128)(2,1)} %copy-done) | copy-start | bytes 786436
  88.3 2.5 %collective-permute-start.2 = (f32[384]{0:T(512)S(1)}, f32[384]{0:T(512)S(1)}, u32[]{:S(2)}, u32[]{:S(2)}) collective-permute-start(f32[384]{0:T(512)S(1)} %slice.105), channel_id=1, source_target_pairs={{4,0},{8,4},{12,8},{16,12},{20,16},{24,20},{28,24},{32,28},{36,32}... | collective-permute-start | bytes 4616 | tf_op jit(solution)/shard_map/ppermute | solution.py:14
  90.8 6.9 %collective-permute-start.3 = (f32[384]{0:T(512)S(1)}, f32[384]{0:T(512)S(1)}, u32[]{:S(2)}, u32[]{:S(2)}) collective-permute-start(f32[384]{0:T(512)S(1)} %slice_add_fusion.1), channel_id=1, source_target_pairs={{4,0},{8,4},{12,8},{16,12},{20,16},{24,20},{28,24},{32,28},{36,32}... | collective-permute-start | bytes 4616 | tf_op jit(solution)/shard_map/ppermute | solution.py:14
where the time goes:
time: 109 us
  waiting for transfers between devices  31.8 us (29%)
  starting transfers between devices  18.9 us (17%)
  matrix products  18.1 us (17%)
  local copies, waits for them, and re-layouts  15.1 us (14%)
  other arithmetic  13.5 us (12%)
  blocking collectives  10.6 us (10%)
    ppermute x4, waiting for transfers between devices, passed_along(): return lax.ppermute(block, axis, route)  31.8 us
    all_to_all x1, starting transfers between devices, on_device(): lax.all_to_all(outgoing, 'ctx', split_axis=1, concat_axis=1, tiled=True)  13.5 us
    psum x1, blocking collectives, on_device(): carry = lax.psum(carry, 'head')  10.6 us
    dot_general x4, matrix products, on_device(): jnp.einsum('qrd,kd->rqk', query_g, key_g, preferred_element_type=jnp.floa...  10.6 us
    reduce_sum x4, other arithmetic, on_device(): total = jnp.sum(weight, -1, keepdims=True)  7.96 us
    dot_general x4, matrix products, on_device(): jnp.einsum('rqk,kd->qrd', weight.astype(jnp.bfloat16), val_g, preferred_e...  7.52 us
    unnamed x9, local copies, waits for them, and re-layouts  6.39 us
    ppermute x4, starting transfers between devices, passed_along(): return lax.ppermute(block, axis, route)  5.4 us
  transfers between devices with their start and end apart: 5, of which 3 were waited for; matrix products, arithmetic and copies ran while one was open for 5% of the time, Pallas kernels for 0%

commit v1 on v0

v1 whole, which is shorter than its diff:
```python
import jax
import jax.numpy as jnp
from jax import lax
from jax.experimental import pallas as pl
from jax.experimental.pallas import tpu as pltpu
from jax.sharding import PartitionSpec as P

HD = 128
KB = 4
QH = 64
TOK = 384
HALF = 192
G = 2
QPK = 8
HEADS = G * QPK
N_CTX = 64
F32 = jnp.float32
BF = jnp.bfloat16
LOG2E_SCALE = HD**-0.5 * 1.4426950408889634
MESH = pl.DeviceIdType.MESH


def dot(a, b):
    return lax.dot_general(a, b, (((1,), (0,)), ((), ())), preferred_element_type=F32)


def dot_t(a, b):
    return lax.dot_general(a, b, (((1,), (1,)), ((), ())), preferred_element_type=F32)


def iota(shape, dim):
    return lax.broadcasted_iota(jnp.int32, shape, dim)


def with_ones(v):
    return jnp.concatenate([v, jnp.ones(v.shape, BF)], 1)


def column_sum(w, f):
    r, n = w.shape
    return jnp.sum((w.astype(F32) * f[:, :1]).reshape(r // 8, 8, n), 0)


def emit(units, skew):
    stages = max(len(u) for u in units)
    for t in range(len(units) + (stages - 1) * skew):
        for k in range(stages):
            i = t - k * skew
            if 0 <= i < len(units) and k < len(units[i]):
                units[i][k]()


def kernel(
    q_hbm, k_hbm, v_hbm, rows_hbm, dest_hbm, count_hbm,
    out_hbm, score_hbm, cache_hbm,
    q_ref, k_ref, v_ref, rows_ref, dest_ref, count_ref,
    kn_ref, vn_ref, stage, outgoing, plane, out_ref,
    ot1, m1, wl, wh, col_own, col_near, col_send, col_recv, score_ref,
    in_sem, out_sem, kv_send, kv_recv, p1_send, p1_recv, p2_send, p2_recv, ks_send, ks_recv,
):
    c = lax.axis_index("ctx")
    hd = lax.axis_index("head")
    x = lax.div(c, 16)
    z = lax.rem(lax.div(c, 2), 8)
    y = lax.rem(c, 2)
    xy = x * 2 + y

    def ctx(delta):
        return lax.rem(c + delta + N_CTX, N_CTX)

    def xy_ctx(i):
        p = lax.rem(xy + i + 8, 8)
        return p, lax.div(p, 2) * 16 + z * 2 + lax.rem(p, 2)

    def z_ctx(i):
        p = lax.rem(z + i + 8, 8)
        return p, x * 16 + p * 2 + y

    def head_of(i):
        return lax.rem(hd + i, 4)

    loads = [
        pltpu.make_async_copy(src, dst, in_sem.at[i])
        for i, (src, dst) in enumerate(
            [
                (k_hbm, k_ref), (v_hbm, v_ref), (rows_hbm, rows_ref), (dest_hbm, dest_ref),
                (count_hbm, count_ref),
                (q_hbm.at[:, pl.ds(0, QPK * HD)], q_ref.at[:, pl.ds(0, QPK * HD)]),
                (q_hbm.at[:, pl.ds(QPK * HD, QPK * HD)], q_ref.at[:, pl.ds(QPK * HD, QPK * HD)]),
            ]
        )
    ]
    for load in loads:
        load.start()

    barrier = pltpu.get_barrier_semaphore()
    greeted = [(ctx(-1), hd), (ctx(-2), hd)]
    greeted += [(xy_ctx(i)[1], hd) for i in range(1, 8)]
    greeted += [(z_ctx(i)[1], hd) for i in range(1, 8)]
    greeted += [(ctx(1), head_of(i)) for i in range(4)]
    greeted += [(ctx(2), head_of(i)) for i in range(4)]
    greeted += [(c, head_of(i)) for i in range(1, 4)]
    for a, b in greeted:
        pl.semaphore_signal(barrier, inc=1, device_id={"ctx": a, "head": b}, device_id_type=MESH)

    for load in loads[:2]:
        load.wait()
    pl.semaphore_wait(barrier, len(greeted))

    def kv_copy(which, slot, rows, delta):
        src = (k_ref, v_ref)[which].at[pl.ds(rows, HALF)]
        dst = (kn_ref, vn_ref)[which].at[pl.ds(slot * HALF, HALF)]
        return pltpu.make_async_remote_copy(
            src_ref=src, dst_ref=dst,
            send_sem=kv_send.at[which, slot], recv_sem=kv_recv.at[which, slot],
            device_id={"ctx": ctx(delta), "head": hd}, device_id_type=MESH,
        )

    near_a = [kv_copy(w, 0, 0, 1) for w in range(2)]
    near_b = [kv_copy(w, 1, 0, 2) for w in range(2)]
    far_b = [kv_copy(w, 2, HALF, 2) for w in range(2)]
    far_a = [kv_copy(w, 3, HALF, 1) for w in range(2)]
    for w in range(2):
        near_a[w].start()
        near_b[w].start()

    @pl.when(c >= N_CTX - 2)
    def _():
        for copy in far_b:
            copy.start()

    @pl.when(c == N_CTX - 1)
    def _():
        for copy in far_a:
            copy.start()

    for load in loads[2:5]:
        load.wait()
    d = iota((N_CTX, N_CTX), 0)
    order = (d >> 4) * 16 + (d & 7) * 2 + ((d >> 3) & 1)
    lane = iota((N_CTX, TOK), 1).astype(F32)
    for g in range(G):
        match = dest_ref[0, g : g + 1, :] == order
        live = jnp.sum(
            jnp.where(match, count_ref[0, g : g + 1, :].astype(F32), 0.0), 1, keepdims=True
        )
        match = jnp.where(match, 1.0, 0.0).astype(BF)
        rows = rows_ref[0, g]
        high = dot(match, (rows >> 4).astype(F32).astype(BF))
        low = dot(match, (rows & 15).astype(F32).astype(BF))
        rows = high * 16.0 + low
        pair = jnp.concatenate(
            [k_ref[:, g * HD : (g + 1) * HD], v_ref[:, g * HD : (g + 1) * HD]], 1
        )
        for t in range(KB):
            row = jnp.where(live > t, rows[:, t : t + 1], -1.0)
            pick = jnp.where(row == lane, 1.0, 0.0).astype(BF)
            picked = dot(pick, pair)
            for half in range(2):
                stage[pl.ds(t * 4 + half * 2 + g, N_CTX, stride=16), :] = picked[
                    :, half * HD : (half + 1) * HD
                ]
    for i in range(8):
        outgoing[i] = stage[i * 128 : (i + 1) * 128].astype(BF)

    phase1 = []
    for i in range(1, 8):
        p, there = xy_ctx(i)
        phase1.append(
            pltpu.make_async_remote_copy(
                src_ref=outgoing.at[p], dst_ref=plane.at[x, y],
                send_sem=p1_send.at[i - 1], recv_sem=p1_recv.at[i - 1],
                device_id={"ctx": there, "head": hd}, device_id_type=MESH,
            )
        )
    for copy in phase1:
        copy.start()
    plane[x, y] = outgoing[xy]

    mask_l = iota((HALF, 256), 1) <= iota((HALF, 256), 0)
    mask_h = iota((HALF, TOK), 1) <= iota((HALF, TOK), 0) + HALF

    def own_part(g, h, part):
        qs = pl.multiple_of(h * HD, HD)
        low = part == 0
        rs = slice(0, HALF) if low else slice(HALF, TOK)
        n = 256 if low else TOK
        st = {}

        def first():
            s = dot_t(q_ref[rs, pl.ds(qs, HD)], k_ref[:n, g * HD : (g + 1) * HD])
            st["s"] = jnp.where(mask_l if low else mask_h, s, -jnp.inf)
            st["m"] = jnp.max(st["s"], 1, keepdims=True)

        def second():
            w = jnp.exp2((st["s"] - st["m"]) * LOG2E_SCALE).astype(BF)
            (wl if low else wh)[h] = w
            m1[h, rs] = jnp.broadcast_to(st["m"], (HALF, HD))
            ot1[h, rs] = dot(w, with_ones(v_ref[:n, g * HD : (g + 1) * HD]))

        return [first, second]

    for g in range(G):
        loads[5 + g].wait()

        def own_heads(i, carry, g=g):
            units = []
            for u in range(4):
                h = g * QPK + i * 4 + u
                units += [own_part(g, h, 0), own_part(g, h, 1)]
            emit(units, 2)
            return carry

        lax.fori_loop(0, QPK // 4, own_heads, 0)

    for i in range(1, 8):
        p, _ = xy_ctx(-i)
        pltpu.make_async_remote_copy(
            src_ref=outgoing.at[p], dst_ref=plane.at[lax.div(p, 2), lax.rem(p, 2)],
            send_sem=p1_send.at[i - 1], recv_sem=p1_recv.at[i - 1],
            device_id={"ctx": xy_ctx(-i)[1], "head": hd}, device_id_type=MESH,
        ).wait_recv()
    phase2 = []
    for i in range(1, 8):
        p, there = z_ctx(i)
        phase2.append(
            pltpu.make_async_remote_copy(
                src_ref=plane.at[:, :, pl.ds(pl.multiple_of(p * 16, 16), 16), :],
                dst_ref=cache_hbm.at[:, z],
                send_sem=p2_send.at[i - 1], recv_sem=p2_recv.at[i - 1],
                device_id={"ctx": there, "head": hd}, device_id_type=MESH,
            )
        )
    for copy in phase2:
        copy.start()
    cache_own = pltpu.make_async_copy(
        plane.at[:, :, pl.ds(pl.multiple_of(z * 16, 16), 16), :], cache_hbm.at[:, z], out_sem.at[2]
    )
    cache_own.start()

    for w in range(2):
        near_a[w].wait_recv()
        near_b[w].wait_recv()

    out_copies = [
        pltpu.make_async_copy(
            out_ref.at[:, pl.ds(g * QPK * HD, QPK * HD)],
            out_hbm.at[:, pl.ds(g * QPK * HD, QPK * HD)],
            out_sem.at[g],
        )
        for g in range(G)
    ]

    def near_part(g, h, rs, n, acc):
        qs = pl.multiple_of(h * HD, HD)
        st = {}

        def first():
            if n:
                st["s"] = dot_t(q_ref[rs, pl.ds(qs, HD)], kn_ref[:n, g * HD : (g + 1) * HD])
                st["m"] = jnp.maximum(m1[h, rs], jnp.max(st["s"], 1, keepdims=True))

        def second():
            if n:
                w = jnp.exp2((st["s"] - st["m"][:, :1]) * LOG2E_SCALE).astype(BF)
                st["w"] = w
                st["ot"] = dot(w, with_ones(vn_ref[:n, g * HD : (g + 1) * HD]))

        def third():
            o1 = ot1[h, rs]
            if n:
                a = jnp.exp2((m1[h, rs] - st["m"]) * LOG2E_SCALE)
                inv = 1.0 / (a * o1[:, HD:] + st["ot"][:, HD:])
                o = (a * o1[:, :HD] + st["ot"][:, :HD]) * inv
                f = a * inv
                s = column_sum(st["w"], inv)
                for i in range(0, n, TOK):
                    part = s[:, i : min(i + TOK, n)]
                    if part.shape[1] < TOK:
                        part = jnp.concatenate(
                            [part, jnp.zeros((8, TOK - part.shape[1]), F32)], 1
                        )
                    acc[1 + i // TOK] = acc[1 + i // TOK] + part
            else:
                f = 1.0 / o1[:, HD:]
                o = o1[:, :HD] * f
            out_ref[rs, pl.ds(qs, HD)] = o.astype(BF)
            if rs.start < HALF:
                s = column_sum(wl[h], f[:HALF])
                acc[0] = acc[0] + jnp.concatenate([s, jnp.zeros((8, TOK - 256), F32)], 1)
            if rs.stop > HALF:
                acc[0] = acc[0] + column_sum(wh[h], f[HALF - rs.start :])

        return [first, second, third]

    def near_attention(parts, unroll):
        zero = jnp.zeros((8, TOK), F32)
        carry = (zero, zero, zero)
        for g in range(G):

            def heads(i, carry, g=g):
                acc = list(carry)
                units = []
                for u in range(unroll):
                    for rs, n in parts:
                        units.append(near_part(g, g * QPK + i * unroll + u, rs, n, acc))
                emit(units, 0)
                return tuple(acc)

            carry = lax.fori_loop(0, QPK // unroll, heads, carry)
            out_copies[g].start()
        col_own[...] = carry[0]
        col_near[0] = carry[1]
        col_near[1] = carry[2]

    @pl.when(c >= 2)
    def _():
        near_attention([(slice(0, TOK), TOK)], 8)

    @pl.when(c == 1)
    def _():
        for copy in far_b:
            copy.wait_recv()
        near_attention([(slice(0, HALF), HALF), (slice(HALF, TOK), 3 * HALF)], 8)

    @pl.when(c == 0)
    def _():
        for copy in far_b + far_a:
            copy.wait_recv()
        near_attention([(slice(0, HALF), 0), (slice(HALF, TOK), 4 * HALF)], 8)

    first = jnp.sum(col_near[0], 0, keepdims=True)
    second = jnp.sum(col_near[1], 0, keepdims=True)
    low = iota((1, TOK), 1) < HALF
    col_send[0] = jnp.sum(col_own[...], 0, keepdims=True)
    col_send[1] = jnp.where(low, first, second)
    col_send[2] = pltpu.roll(jnp.where(low, second, first), HALF, 1)
    sends = []
    for delta in range(3):
        for i in range(4):
            if delta or i:
                sends.append(
                    pltpu.make_async_remote_copy(
                        src_ref=col_send.at[delta], dst_ref=col_recv.at[delta * 4 + i],
                        send_sem=ks_send.at[delta * 4 + i], recv_sem=ks_recv.at[delta * 4 + i],
                        device_id={"ctx": ctx(-delta), "head": head_of(i)}, device_id_type=MESH,
                    )
                )
    for copy in sends:
        copy.start()
    for copy in sends:
        copy.wait_recv()
    total = col_send[0]
    for i in range(1, 12):
        total = total + col_recv[i]
    score_ref[...] = total * (1.0 / QH)
    score_copy = pltpu.make_async_copy(score_ref, score_hbm, out_sem.at[3])
    score_copy.start()

    for copy in phase2:
        copy.wait_send()
    for i in range(1, 8):
        p, there = z_ctx(-i)
        pltpu.make_async_remote_copy(
            src_ref=plane.at[:, :, pl.ds(pl.multiple_of(p * 16, 16), 16), :],
            dst_ref=cache_hbm.at[:, p],
            send_sem=p2_send.at[i - 1], recv_sem=p2_recv.at[i - 1],
            device_id={"ctx": there, "head": hd}, device_id_type=MESH,
        ).wait_recv()
    for copy in near_a + near_b + phase1 + sends:
        copy.wait_send()

    @pl.when(c >= N_CTX - 2)
    def _():
        for copy in far_b:
            copy.wait_send()

    @pl.when(c == N_CTX - 1)
    def _():
        for copy in far_a:
            copy.wait_send()

    for copy in out_copies + [cache_own, score_copy]:
        copy.wait()


def on_device(queries, keys, values, keep_rows, keep_dest, keep_count):
    anyspace = pl.BlockSpec(memory_space=pl.ANY)
    dma = pltpu.SemaphoreType.DMA
    attended, scores, cache = pl.pallas_call(
        kernel,
        name="window",
        out_shape=[
            jax.ShapeDtypeStruct((TOK, HEADS * HD), BF),
            jax.ShapeDtypeStruct((1, TOK), F32),
            jax.ShapeDtypeStruct((4, 8, 2, 16, HD), BF),
        ],
        in_specs=[anyspace] * 6,
        out_specs=[anyspace] * 3,
        scratch_shapes=[
            pltpu.VMEM((TOK, HEADS * HD), BF),
            pltpu.VMEM((TOK, G * HD), BF),
            pltpu.VMEM((TOK, G * HD), BF),
            pltpu.VMEM((1, G, N_CTX, KB), jnp.int32),
            pltpu.VMEM((1, G, N_CTX), jnp.int32),
            pltpu.VMEM((1, G, N_CTX), jnp.int32),
            pltpu.VMEM((4 * HALF, G * HD), BF),
            pltpu.VMEM((4 * HALF, G * HD), BF),
            pltpu.VMEM((N_CTX * 16, HD), F32),
            pltpu.VMEM((8, 128, HD), BF),
            pltpu.VMEM((4, 2, 128, HD), BF),
            pltpu.VMEM((TOK, HEADS * HD), BF),
            pltpu.VMEM((HEADS, TOK, 2 * HD), F32),
            pltpu.VMEM((HEADS, TOK, HD), F32),
            pltpu.VMEM((HEADS, HALF, 256), BF),
            pltpu.VMEM((HEADS, HALF, TOK), BF),
            pltpu.VMEM((8, TOK), F32),
            pltpu.VMEM((2, 8, TOK), F32),
            pltpu.VMEM((3, 1, TOK), F32),
            pltpu.VMEM((12, 1, TOK), F32),
            pltpu.VMEM((1, TOK), F32),
            dma((7,)), dma((4,)),
            dma((2, 4)), dma((2, 4)),
            dma((7,)), dma((7,)), dma((7,)), dma((7,)),
            dma((12,)), dma((12,)),
        ],
        compiler_params=pltpu.CompilerParams(
            collective_id=0, has_side_effects=True, vmem_limit_bytes=40 << 20
        ),
        cost_estimate=pl.CostEstimate(
            flops=2_200_000_000, bytes_accessed=4_000_000, transcendentals=4_200_000
        ),
    )(queries, keys, values, keep_rows, keep_dest, keep_count)
    cache = cache.reshape(N_CTX, KB, 2, G, HD).transpose(0, 1, 3, 2, 4)
    return attended, scores.reshape(TOK), cache.reshape(1, N_CTX, KB, G, 2 * HD)


def solution(mesh):
    return jax.shard_map(
        on_device,
        mesh=mesh,
        in_specs=(
            P("ctx", "head"),
            P("ctx", "head"),
            P("ctx", "head"),
            P("ctx", "head", None, None),
            P("ctx", "head", None),
            P("ctx", "head", None),
        ),
        out_specs=(P("ctx", "head"), P("ctx"), P("ctx", None, None, "head", None)),
        check_vma=False,
    )
```

time: 109 us -> 55 us (0.50)
  Pallas kernels: 0 us -> 46.3 us
  waiting for transfers between devices: 31.8 us -> 0 us
  starting transfers between devices: 18.9 us -> 0 us
  matrix products: 18.1 us -> 0 us
  other arithmetic: 13.5 us -> 0.6 us
  blocking collectives: 10.6 us -> 0 us
  local copies, waits for them, and re-layouts: 15.1 us -> 7.24 us
    pallas_call x0 -> x1, Pallas kernels: none -> 46.3 us  [on_device(): pl.pallas_call(kernel, name='window', out_shape=[jax.ShapeDtypeStruct((TO...]
    ppermute x4 -> x0, waiting for transfers between devices: 31.8 us -> none  [passed_along(): return lax.ppermute(block, axis, route)]
    dot_general x8 -> x0, matrix products: 18.1 us -> none  [the longest x4 10.6 us: on_device(): jnp.einsum('qrd,kd->rqk', query_g, key_g, preferred_element_type=jnp.floa...]
    all_to_all x1 -> x0, starting transfers between devices: 13.5 us -> none  [on_device(): lax.all_to_all(outgoing, 'ctx', split_axis=1, concat_axis=1, tiled=True)]
    reduce_sum x7 -> x0, other arithmetic: 11.7 us -> none  [the longest x4 7.96 us: on_device(): total = jnp.sum(weight, -1, keepdims=True)]
    psum x1 -> x0, blocking collectives: 10.6 us -> none  [on_device(): carry = lax.psum(carry, 'head')]
    ppermute x4 -> x0, starting transfers between devices: 5.4 us -> none  [passed_along(): return lax.ppermute(block, axis, route)]
    gather x4 -> x0, local copies, waits for them, and re-layouts: 3.69 us -> none  [the longest x2 2.3 us: on_device(): jnp.take(pair[:, group], rows_g.reshape(-1), axis=0)]
  transfers between devices with their start and end apart: 5 -> 0, of which waited for: 3 -> 0; matrix products, arithmetic and copies ran while one was open for 5% -> 0% of each run, Pallas kernels for 0% -> 0%
where the time goes in v1:
time: 55 us; the launch traced here: 54.8 us
  Pallas kernels  46.3 us (84%)
  local copies, waits for them, and re-layouts  7.24 us (13%)
  between operations  0.66 us (1%)
  other arithmetic  0.6 us (1%)
    pallas_call x1, Pallas kernels, on_device(): pl.pallas_call(kernel, name='window', out_shape=[jax.ShapeDtypeStruct((TO...  46.3 us
    unnamed x13, local copies, waits for them, and re-layouts  7.24 us

profile of v1, /device:TPU:1, one launch (start us, length us, event | category | flops | bytes accessed | tf_op | source)
XLA Modules:
  0.0 54.8 jit_solution(8861699063283568791)
XLA Ops:
  0.6 0.8 %copy.9.rows_hbm = s32[1,2,64,4]{3,2,1,0:T(8,128)S(1)} copy(s32[1,2,64,4]{2,3,1,0:T(4,128)} %param.9) | data formatting | bytes 4096 | tf_op args[3]
  1.4 0.0 copy-start
  1.4 1.4 %copy-done = bf16[384,2048]{1,0:T(8,128)(2,1)S(1)} copy-done((bf16[384,2048]{1,0:T(8,128)(2,1)S(1)}, bf16[384,2048]{1,0:T(8,128)(2,1)}, u32[]{:S(2)}) %copy-start) | copy-done | bytes 1572888
  2.8 0.0 copy-start.1
  2.8 0.9 %copy-done.1 = bf16[384,256]{1,0:T(8,128)(2,1)S(1)} copy-done((bf16[384,256]{1,0:T(8,128)(2,1)S(1)}, bf16[384,256]{1,0:T(8,128)(2,1)}, u32[]{:S(2)}) %copy-start.1) | copy-done | bytes 196632
  3.8 0.0 copy-start.2
  3.8 0.9 %copy-done.2 = bf16[384,256]{1,0:T(8,128)(2,1)S(1)} copy-done((bf16[384,256]{1,0:T(8,128)(2,1)S(1)}, bf16[384,256]{1,0:T(8,128)(2,1)}, u32[]{:S(2)}) %copy-start.2) | copy-done | bytes 196632
  4.7 0.0 copy-start.3
  4.7 0.7 %copy-done.3 = s32[1,2,64]{2,1,0:T(2,128)S(1)} copy-done((s32[1,2,64]{2,1,0:T(2,128)S(1)}, s32[1,2,64]{2,1,0:T(2,128)}, u32[]{:S(2)}) %copy-start.3) | copy-done | bytes 536
  5.4 0.0 copy-start.4
  5.4 0.7 %copy-done.4 = s32[1,2,64]{2,1,0:T(2,128)S(1)} copy-done((s32[1,2,64]{2,1,0:T(2,128)S(1)}, s32[1,2,64]{2,1,0:T(2,128)}, u32[]{:S(2)}) %copy-start.4) | copy-done | bytes 536
  6.0 46.3 %window.1 = (bf16[384,2048]{1,0:T(8,128)(2,1)S(1)}, f32[1,384]{1,0:T(1,128)S(1)}, bf16[4,8,2,16,128]{4,3,2,1,0:T(8,128)(2,1)S(1)}) custom-call(bf16[384,2048]{1,0:T(8,128)(2,1)S(1)} %copy-done, bf16[384,256]{1,0:T(8,128)(2,1)S(1)} %copy-done.1, bf16[384,256]{1,0:T(8,128)(2,1)S(1)} %copy-done.2, s32[1,2,64,4]{3,2,1,0:T(8,128)S(1)} %copy.9.rows_hbm, ...), custom_call_target="tpu_custom_call" | custom-call | flops 2200000000 | bytes 4000000 | tf_op jit(solution)/shard_map/window/pallas_call | solution.py:390
  52.3 0.6 %reduce = f32[384]{0:T(512)} reduce(f32[1,384]{1,0:T(1,128)S(1)} %get-tuple-element.7, f32[]{:T(128)} %constant.3), dimensions={0}, to_apply=%get-tuple-element.7.reduce_sub_computation | reduce | bytes 3076 | tf_op jit(solution)/shard_map/window/pallas_call | solution.py:390
  52.9 1.1 %copy.13 = bf16[384,2048]{1,0:T(8,128)(2,1)} copy(bf16[384,2048]{1,0:T(8,128)(2,1)S(1)} %get-tuple-element.12) | data formatting | bytes 3145728
  54.1 0.7 %copy.14 = bf16[1,64,4,2,256]{4,3,2,1,0:T(2,128)(2,1)} copy(bf16[1,64,4,2,256]{4,3,2,1,0:T(2,128)(2,1)S(1)} %bitcast.5) | data formatting | bytes 524288
Async XLA Ops:
  1.4 1.4 %copy-start = (bf16[384,2048]{1,0:T(8,128)(2,1)S(1)}, bf16[384,2048]{1,0:T(8,128)(2,1)}, u32[]{:S(2)}) copy-start(bf16[384,2048]{1,0:T(8,128)(2,1)} %q_hbm.1) | copy-start | bytes 4718596
  2.8 0.9 %copy-start.1 = (bf16[384,256]{1,0:T(8,128)(2,1)S(1)}, bf16[384,256]{1,0:T(8,128)(2,1)}, u32[]{:S(2)}) copy-start(bf16[384,256]{1,0:T(8,128)(2,1)} %k_hbm.1) | copy-start | bytes 589828
  3.8 0.9 %copy-start.2 = (bf16[384,256]{1,0:T(8,128)(2,1)S(1)}, bf16[384,256]{1,0:T(8,128)(2,1)}, u32[]{:S(2)}) copy-start(bf16[384,256]{1,0:T(8,128)(2,1)} %v_hbm.1) | copy-start | bytes 589828
  4.7 0.7 %copy-start.3 = (s32[1,2,64]{2,1,0:T(2,128)S(1)}, s32[1,2,64]{2,1,0:T(2,128)}, u32[]{:S(2)}) copy-start(s32[1,2,64]{2,1,0:T(2,128)} %dest_hbm.1) | copy-start | bytes 1540
  5.4 0.7 %copy-start.4 = (s32[1,2,64]{2,1,0:T(2,128)S(1)}, s32[1,2,64]{2,1,0:T(2,128)}, u32[]{:S(2)}) copy-start(s32[1,2,64]{2,1,0:T(2,128)} %count_hbm.1) | copy-start | bytes 1540

commit v2 on v1

v2 whole, which is shorter than its diff:
```python
import jax
import jax.numpy as jnp
from jax import lax
from jax.experimental import pallas as pl
from jax.experimental.pallas import tpu as pltpu
from jax.sharding import PartitionSpec as P

HD = 128
KB = 4
QH = 64
TOK = 384
HALF = 192
G = 2
QPK = 8
HEADS = G * QPK
N_CTX = 64
F32 = jnp.float32
BF = jnp.bfloat16
LOG2E_SCALE = HD**-0.5 * 1.4426950408889634
MESH = pl.DeviceIdType.MESH


def dot(a, b):
    return lax.dot_general(a, b, (((1,), (0,)), ((), ())), preferred_element_type=F32)


def dot_t(a, b):
    return lax.dot_general(a, b, (((1,), (1,)), ((), ())), preferred_element_type=F32)


def iota(shape, dim):
    return lax.broadcasted_iota(jnp.int32, shape, dim)


def with_ones(v):
    return jnp.concatenate([v, jnp.ones(v.shape, BF)], 1)


def column_sum(w, f):
    r, n = w.shape
    return jnp.sum((w.astype(F32) * f[:, :1]).reshape(r // 8, 8, n), 0)


def emit(units, skew):
    stages = max(len(u) for u in units)
    for t in range(len(units) + (stages - 1) * skew):
        for k in range(stages):
            i = t - k * skew
            if 0 <= i < len(units) and k < len(units[i]):
                units[i][k]()


def kernel(
    q_hbm, k_hbm, v_hbm, rows_hbm, dest_hbm, count_hbm,
    out_ref, score_ref, cache_ref,
    q_ref, k_ref, v_ref, rows_ref, dest_ref, count_ref,
    kn_ref, vn_ref, stage, outgoing,
    ot1, m1, wl, wh, col_own, col_near, col_send, col_recv,
    in_sem, cache_send, cache_recv, kv_send, kv_recv, relay_send,
    ks_send, ks_recv,
):
    c = lax.axis_index("ctx")
    hd = lax.axis_index("head")
    x = lax.div(c, 16)
    z = lax.rem(lax.div(c, 2), 8)
    y = lax.rem(c, 2)
    odd = y == 1
    even = y == 0

    def ctx(delta):
        return lax.rem(c + delta + N_CTX, N_CTX)

    def head_of(i):
        return lax.rem(hd + i, 4)

    barrier = pltpu.get_barrier_semaphore()
    def greet(a, b):
        pl.semaphore_signal(barrier, inc=1, device_id={"ctx": a, "head": b}, device_id_type=MESH)

    def greet_row(i, carry):
        greet(ctx(i), hd)
        return carry

    lax.fori_loop(1, N_CTX, greet_row, 0)
    greeted = N_CTX - 1
    for delta in range(3):
        for i in range(1, 4):
            greet(ctx(delta), head_of(i))
            greeted += 1

    @pl.when(c == 1)
    def _():
        vn_ref[3 * HALF :, :] = jnp.zeros((HALF, G * HD), BF)

    loads = [
        pltpu.make_async_copy(src, dst, in_sem.at[i])
        for i, (src, dst) in enumerate(
            [
                (k_hbm, k_ref), (v_hbm, v_ref), (rows_hbm, rows_ref), (dest_hbm, dest_ref),
                (count_hbm, count_ref),
                (q_hbm.at[:, pl.ds(0, QPK * HD)], q_ref.at[:, pl.ds(0, QPK * HD)]),
                (q_hbm.at[:, pl.ds(QPK * HD, QPK * HD)], q_ref.at[:, pl.ds(QPK * HD, QPK * HD)]),
            ]
        )
    ]
    for load in loads:
        load.start()

    def kv_copy(w, g, slot, row, delta):
        cols = pl.ds(g * HD, HD)
        return pltpu.make_async_remote_copy(
            src_ref=(k_hbm, v_hbm)[w].at[pl.ds(row, HALF), cols],
            dst_ref=(kn_ref, vn_ref)[w].at[pl.ds(slot * HALF, HALF), cols],
            send_sem=kv_send.at[w, g, slot], recv_sem=kv_recv.at[w, g, slot],
            device_id={"ctx": ctx(delta), "head": hd}, device_id_type=MESH,
        )

    def relay_copy(w, g, slot, to):
        cols = pl.ds(g * HD, HD)
        near = (kn_ref, vn_ref)[w]
        return pltpu.make_async_remote_copy(
            src_ref=near.at[pl.ds(slot * HALF, HALF), cols],
            dst_ref=near.at[pl.ds(to * HALF, HALF), cols],
            send_sem=relay_send.at[w, g, slot], recv_sem=kv_recv.at[w, g, to],
            device_id={"ctx": ctx(-1), "head": hd}, device_id_type=MESH,
        )

    send_a = [[kv_copy(w, g, 0, 0, 1) for w in range(2)] for g in range(G)]
    send_b = [[kv_copy(w, g, 1, 0, 2) for w in range(2)] for g in range(G)]
    send_far = [[kv_copy(w, g, 2, HALF, 2) for w in range(2)] for g in range(G)]
    relay_low = [[relay_copy(w, g, 1, 0) for w in range(2)] for g in range(G)]
    relay_high = [[relay_copy(w, g, 2, 3) for w in range(2)] for g in range(G)]

    def send_blocks():
        for g in range(G):
            for copy in send_b[g]:
                copy.start()

            @pl.when(even)
            def _():
                for copy in send_a[g]:
                    copy.start()

            @pl.when(c >= N_CTX - 2)
            def _():
                for copy in send_far[g]:
                    copy.start()

    def relay(g):
        @pl.when(odd)
        def _():
            for w in range(2):
                send_b[g][w].wait_recv()
                relay_low[g][w].start()

        @pl.when(c == 1)
        def _():
            for w in range(2):
                send_far[g][w].wait_recv()
                relay_high[g][w].start()

    def wait_blocks(g):
        @pl.when(even)
        def _():
            for copy in send_b[g]:
                copy.wait_recv()

        for copy in send_a[g]:
            copy.wait_recv()

        @pl.when(c == 0)
        def _():
            for w in range(2):
                send_far[g][w].wait_recv()
                relay_high[g][w].wait_recv()

    def compact():
        for load in loads[:5]:
            load.wait()
        order = iota((N_CTX, N_CTX), 0)
        lane = iota((N_CTX, TOK), 1).astype(F32)
        for g in range(G):
            match = dest_ref[0, g : g + 1, :] == order
            live = jnp.sum(
                jnp.where(match, count_ref[0, g : g + 1, :].astype(F32), 0.0), 1, keepdims=True
            )
            match = jnp.where(match, 1.0, 0.0).astype(BF)
            rows = rows_ref[0, g]
            high = dot_t(match, (rows >> 4).astype(F32).astype(BF))
            low = dot_t(match, (rows & 15).astype(F32).astype(BF))
            rows = high * 16.0 + low
            pair = jnp.concatenate(
                [k_ref[:, g * HD : (g + 1) * HD], v_ref[:, g * HD : (g + 1) * HD]], 1
            )
            for t in range(KB):
                row = jnp.where(live > t, rows[:, t : t + 1], -1.0)
                pick = jnp.where(row == lane, 1.0, 0.0).astype(BF)
                picked = dot(pick, pair)
                for half in range(2):
                    stage[pl.ds(t * 4 + half * 2 + g, N_CTX, stride=16), :] = picked[
                        :, half * HD : (half + 1) * HD
                    ]
        outgoing[...] = stage[...].reshape(N_CTX, 16, HD).astype(BF)

    def send_block(to):
        @pl.when(to != c)
        def _():
            pltpu.make_async_remote_copy(
                src_ref=outgoing.at[to], dst_ref=cache_ref.at[c],
                send_sem=cache_send, recv_sem=cache_recv,
                device_id={"ctx": to, "head": hd}, device_id_type=MESH,
            ).start()

    def send_layer(there):
        def body(i, carry):
            p = lax.rem(x * 2 + y + i, 8)
            send_block(lax.div(p, 2) * 16 + there * 2 + lax.rem(p, 2))
            return carry

        lax.fori_loop(0, 8, body, 0)

    def send_cache():
        send_layer(0)
        for i in range(8):
            there = lax.rem(z + i, 8)

            @pl.when(there != 0)
            def _():
                send_layer(there)

        cache_ref[c] = outgoing[c]

    mask_l = iota((HALF, 256), 1) <= iota((HALF, 256), 0)
    mask_h = iota((HALF, TOK), 1) <= iota((HALF, TOK), 0) + HALF

    def own_part(g, h, part):
        qs = pl.multiple_of(h * HD, HD)
        low = part == 0
        rs = slice(0, HALF) if low else slice(HALF, TOK)
        n = 256 if low else TOK
        st = {}

        def first():
            s = dot_t(q_ref[rs, pl.ds(qs, HD)], k_ref[:n, g * HD : (g + 1) * HD])
            st["s"] = jnp.where(mask_l if low else mask_h, s, -jnp.inf)
            st["m"] = jnp.max(st["s"], 1, keepdims=True)

        def second():
            w = jnp.exp2((st["s"] - st["m"]) * LOG2E_SCALE).astype(BF)
            (wl if low else wh)[h] = w
            m1[h, rs] = jnp.broadcast_to(st["m"], (HALF, HD))
            ot1[h, rs] = dot(w, with_ones(v_ref[:n, g * HD : (g + 1) * HD]))

        return [first, second]

    def own_attention(g):
        loads[5 + g].wait()

        def own_heads(i, carry):
            units = []
            for u in range(4):
                h = g * QPK + i * 4 + u
                units += [own_part(g, h, 0), own_part(g, h, 1)]
            emit(units, 2)
            return carry

        lax.fori_loop(0, QPK // 4, own_heads, 0)

    compact()
    pl.semaphore_wait(barrier, greeted)
    send_blocks()
    send_cache()
    own_attention(0)
    relay(0)
    own_attention(1)

    @pl.when(c != 1)
    def _():
        relay(1)

    def near_part(g, h, rs, live, acc):
        n = (live + 127) // 128 * 128
        qs = pl.multiple_of(h * HD, HD)
        st = {}

        def first():
            if n:
                s = dot_t(q_ref[rs, pl.ds(qs, HD)], kn_ref[:n, g * HD : (g + 1) * HD])
                if live < n:
                    s = jnp.where(iota(s.shape, 1) < live, s, -jnp.inf)
                st["s"] = s
                st["m"] = jnp.maximum(m1[h, rs], jnp.max(st["s"], 1, keepdims=True))

        def second():
            if n:
                w = jnp.exp2((st["s"] - st["m"][:, :1]) * LOG2E_SCALE).astype(BF)
                st["w"] = w
                st["ot"] = dot(w, with_ones(vn_ref[:n, g * HD : (g + 1) * HD]))

        def third():
            o1 = ot1[h, rs]
            if n:
                a = jnp.exp2((m1[h, rs] - st["m"]) * LOG2E_SCALE)
                inv = 1.0 / (a * o1[:, HD:] + st["ot"][:, HD:])
                o = (a * o1[:, :HD] + st["ot"][:, :HD]) * inv
                f = a * inv
                s = column_sum(st["w"], inv)
                for i in range(0, n, TOK):
                    part = s[:, i : min(i + TOK, n)]
                    if part.shape[1] < TOK:
                        part = jnp.concatenate(
                            [part, jnp.zeros((8, TOK - part.shape[1]), F32)], 1
                        )
                    acc[1 + i // TOK] = acc[1 + i // TOK] + part
            else:
                f = 1.0 / o1[:, HD:]
                o = o1[:, :HD] * f
            out_ref[rs, pl.ds(qs, HD)] = o.astype(BF)
            if rs.start < HALF:
                s = column_sum(wl[h], f[:HALF])
                acc[0] = acc[0] + jnp.concatenate([s, jnp.zeros((8, TOK - 256), F32)], 1)
            if rs.stop > HALF:
                acc[0] = acc[0] + column_sum(wh[h], f[HALF - rs.start :])

        return [first, second, third]

    def near_attention(parts, unroll, shard_one=False):
        zero = jnp.zeros((8, TOK), F32)
        carry = (zero, zero, zero)
        for g in range(G):
            if g and shard_one:
                relay(g)
            wait_blocks(g)

            def heads(i, carry, g=g):
                acc = list(carry)
                units = []
                for u in range(unroll):
                    for rs, n in parts:
                        units.append(near_part(g, g * QPK + i * unroll + u, rs, n, acc))
                emit(units, 0)
                return tuple(acc)

            carry = lax.fori_loop(0, QPK // unroll, heads, carry)
        col_own[...] = carry[0]
        col_near[0] = carry[1]
        col_near[1] = carry[2]

    @pl.when(c >= 2)
    def _():
        near_attention([(slice(0, TOK), TOK)], 8)

    @pl.when(c == 1)
    def _():
        near_attention([(slice(0, HALF), HALF), (slice(HALF, TOK), 3 * HALF)], 8, True)

    @pl.when(c == 0)
    def _():
        near_attention([(slice(0, HALF), 0), (slice(HALF, TOK), 4 * HALF)], 8)

    first = jnp.sum(col_near[0], 0, keepdims=True)
    second = jnp.sum(col_near[1], 0, keepdims=True)
    low = iota((1, TOK), 1) < HALF
    col_send[0] = jnp.sum(col_own[...], 0, keepdims=True)
    col_send[1] = jnp.where(low, first, second)
    col_send[2] = pltpu.roll(jnp.where(low, second, first), HALF, 1)
    sends = []
    for delta in range(3):
        for i in range(4):
            if delta or i:
                sends.append(
                    pltpu.make_async_remote_copy(
                        src_ref=col_send.at[delta], dst_ref=col_recv.at[delta * 4 + i],
                        send_sem=ks_send.at[delta * 4 + i], recv_sem=ks_recv.at[delta * 4 + i],
                        device_id={"ctx": ctx(-delta), "head": head_of(i)}, device_id_type=MESH,
                    )
                )
    for copy in sends:
        copy.start()
    for copy in sends:
        copy.wait_recv()
    total = col_send[0]
    for i in range(1, 12):
        total = total + col_recv[i]
    score_ref[...] = total * (1.0 / QH)

    others = cache_ref.at[pl.ds(0, N_CTX - 1)]
    pltpu.make_async_copy(others, others, cache_recv).wait()
    pltpu.make_async_copy(others, others, cache_send).wait()
    for copy in sends:
        copy.wait_send()
    for g in range(G):
        for copy in send_b[g]:
            copy.wait_send()

        @pl.when(even)
        def _():
            for copy in send_a[g]:
                copy.wait_send()

        @pl.when(odd)
        def _():
            for copy in relay_low[g]:
                copy.wait_send()

        @pl.when(c >= N_CTX - 2)
        def _():
            for copy in send_far[g]:
                copy.wait_send()

        @pl.when(c == 1)
        def _():
            for copy in relay_high[g]:
                copy.wait_send()


def tail(a_in, s_in, c_in, a_out, s_out, c_out, sem):
    copies = [
        pltpu.make_async_copy(a_in, a_out, sem.at[0]),
        pltpu.make_async_copy(c_in, c_out, sem.at[1]),
        pltpu.make_async_copy(s_in.at[0], s_out, sem.at[2]),
    ]
    for copy in copies:
        copy.start()
    for copy in copies:
        copy.wait()


def on_device(queries, keys, values, keep_rows, keep_dest, keep_count):
    dma = pltpu.SemaphoreType.DMA
    anywhere = pl.BlockSpec(memory_space=pl.ANY)
    operands = [queries, keys, values, keep_rows.transpose(0, 1, 3, 2), keep_dest, keep_count]
    results = pl.pallas_call(
        lambda *refs: kernel(*refs),
        name="window",
        out_shape=[
            jax.ShapeDtypeStruct((TOK, HEADS * HD), BF),
            jax.ShapeDtypeStruct((1, TOK), F32),
            jax.ShapeDtypeStruct((N_CTX, 16, HD), BF),
        ],
        in_specs=[anywhere] * 6,
        out_specs=[pl.BlockSpec(memory_space=pltpu.VMEM)] * 3,
        scratch_shapes=[
            pltpu.VMEM((TOK, HEADS * HD), BF),
            pltpu.VMEM((TOK, G * HD), BF),
            pltpu.VMEM((TOK, G * HD), BF),
            pltpu.VMEM((1, G, KB, N_CTX), jnp.int32),
            pltpu.VMEM((1, G, N_CTX), jnp.int32),
            pltpu.VMEM((1, G, N_CTX), jnp.int32),
            pltpu.VMEM((4 * HALF, G * HD), BF),
            pltpu.VMEM((4 * HALF, G * HD), BF),
            pltpu.VMEM((N_CTX * 16, HD), F32),
            pltpu.VMEM((N_CTX, 16, HD), BF),
            pltpu.VMEM((HEADS, TOK, 2 * HD), F32),
            pltpu.VMEM((HEADS, TOK, HD), F32),
            pltpu.VMEM((HEADS, HALF, 256), BF),
            pltpu.VMEM((HEADS, HALF, TOK), BF),
            pltpu.VMEM((8, TOK), F32),
            pltpu.VMEM((2, 8, TOK), F32),
            pltpu.VMEM((3, 1, TOK), F32),
            pltpu.VMEM((12, 1, TOK), F32),
            dma((7,)), dma, dma,
            dma((2, G, 4)), dma((2, G, 4)), dma((2, G, 4)),
            dma((12,)), dma((12,)),
        ],
        compiler_params=pltpu.CompilerParams(
            collective_id=0, has_side_effects=True, vmem_limit_bytes=40 << 20
        ),
        cost_estimate=pl.CostEstimate(
            flops=2_200_000_000, bytes_accessed=4_000_000, transcendentals=4_200_000
        ),
    )(*[pltpu.with_memory_space_constraint(v, pltpu.HBM) for v in operands])
    attended, scores, cache = pl.pallas_call(
        tail,
        name="tail",
        out_shape=[
            jax.ShapeDtypeStruct((TOK, HEADS * HD), BF),
            jax.ShapeDtypeStruct((TOK,), F32),
            jax.ShapeDtypeStruct((N_CTX, 16, HD), BF),
        ],
        in_specs=[anywhere] * 3,
        out_specs=[anywhere] * 3,
        scratch_shapes=[dma((3,))],
        compiler_params=pltpu.CompilerParams(vmem_limit_bytes=1 << 20),
    )(*results)
    cache = cache.reshape(N_CTX, KB, 2, G, HD).transpose(0, 1, 3, 2, 4)
    return attended, scores, cache.reshape(1, N_CTX, KB, G, 2 * HD)


def solution(mesh):
    return jax.shard_map(
        on_device,
        mesh=mesh,
        in_specs=(
            P("ctx", "head"),
            P("ctx", "head"),
            P("ctx", "head"),
            P("ctx", "head", None, None),
            P("ctx", "head", None),
            P("ctx", "head", None),
        ),
        out_specs=(P("ctx", "head"), P("ctx"), P("ctx", None, None, "head", None)),
        check_vma=False,
    )
```

time: 55 us -> 45.1 us (0.82)
  local copies, waits for them, and re-layouts: 7.24 us -> 0 us
  Pallas kernels: 46.3 us -> 44.2 us
  other arithmetic: 0.6 us -> 0 us
    unnamed x13 -> x0, local copies, waits for them, and re-layouts: 7.24 us -> none
    pallas_call x1 -> x2, Pallas kernels: 46.3 us -> 44.2 us  [the longest x1 43 us: on_device(): pl.pallas_call(lambda *refs: kernel(*refs), name='window', out_shape=[jax...]
    pallas_call x1 -> x0, other arithmetic: 0.6 us -> none  [on_device(): pl.pallas_call(kernel, name='window', out_shape=[jax.ShapeDtypeStruct((TO...]
where the time goes in v2:
time: 45.1 us; the launch traced here: 45 us
  Pallas kernels  44.2 us (98%)
  between operations  0.82 us (2%)
    pallas_call x1, Pallas kernels, on_device(): pl.pallas_call(lambda *refs: kernel(*refs), name='window', out_shape=[jax...  43 us
    pallas_call x1, Pallas kernels, on_device(): pl.pallas_call(tail, name='tail', out_shape=[jax.ShapeDtypeStruct((TOK, H...  1.25 us

profile of v2, /device:TPU:1, one launch (start us, length us, event | category | flops | bytes accessed | tf_op | source)
XLA Modules:
  0.0 45.0 jit_solution(5309880079239188901)
XLA Ops:
  0.6 43.0 %window.1 = (bf16[384,2048]{1,0:T(8,128)(2,1)S(1)}, f32[1,384]{1,0:T(1,128)S(1)}, bf16[64,16,128]{2,1,0:T(8,128)(2,1)S(1)}) custom-call(bf16[384,2048]{1,0:T(8,128)(2,1)} %refs_0_.1, bf16[384,256]{1,0:T(8,128)(2,1)} %refs_1_.1, bf16[384,256]{1,0:T(8,128)(2,1)} %refs_2_.1, s32[1,2,4,64]{3,2,1,0:T(4,128)} %bitcast.7, s32[1,2,64]{2,1,0:T(2,128)} %refs_4_.1, ...), custom_call_target="tpu_custom_call" | custom-call | flops 2200000000 | bytes 4000000 | tf_op jit(solution)/shard_map/window/pallas_call | solution.py:433
  43.6 1.3 %tail.1 = (bf16[384,2048]{1,0:T(8,128)(2,1)}, f32[384]{0:T(512)}, bf16[64,16,128]{2,1,0:T(8,128)(2,1)}) custom-call(bf16[384,2048]{1,0:T(8,128)(2,1)S(1)} %get-tuple-element.9.a_in, f32[1,384]{1,0:T(1,128)S(1)} %get-tuple-element.10.s_in, bf16[64,16,128]{2,1,0:T(8,128)(2,1)S(1)} %get-tuple-element.11.c_in), custom_call_target="tpu_custom_call" | custom-call | tf_op jit(solution)/shard_map/tail/pallas_call | solution.py:473

commit v3 on v2

--- a/solution.py
+++ b/solution.py
@@ -18,6 +18,7 @@
 BF = jnp.bfloat16
 LOG2E_SCALE = HD**-0.5 * 1.4426950408889634
 MESH = pl.DeviceIdType.MESH
+UNROLL = 8
 
 
 def dot(a, b):
@@ -54,9 +55,9 @@
     q_hbm, k_hbm, v_hbm, rows_hbm, dest_hbm, count_hbm,
     out_ref, score_ref, cache_ref,
     q_ref, k_ref, v_ref, rows_ref, dest_ref, count_ref,
-    kn_ref, vn_ref, stage, outgoing,
-    ot1, m1, wl, wh, col_own, col_near, col_send, col_recv,
-    in_sem, cache_send, cache_recv, kv_send, kv_recv, relay_send,
+    kn_ref, vn_ref, detour_ref, stage, outgoing,
+    ot1, m1, m2, wl, wh, wm, col_send, col_recv,
+    in_sem, cache_send, cache_recv, kv_send, kv_recv, relay_send, detour_send, detour_recv,
     ks_send, ks_recv,
 ):
     c = lax.axis_index("ctx")
@@ -90,7 +91,8 @@
 
     @pl.when(c == 1)
     def _():
-        vn_ref[3 * HALF :, :] = jnp.zeros((HALF, G * HD), BF)
+        kn_ref[2 * HALF - 256 : HALF, :] = jnp.zeros((256 - HALF, G * HD), BF)
+        vn_ref[2 * HALF - 256 : HALF, :] = jnp.zeros((256 - HALF, G * HD), BF)
 
     loads = [
         pltpu.make_async_copy(src, dst, in_sem.at[i])
@@ -115,6 +117,17 @@
             device_id={"ctx": ctx(delta), "head": hd}, device_id_type=MESH,
         )
 
+    def detour_copy(w, first):
+        cols = pl.ds((G - 1) * HD, HD)
+        rows = pl.ds(HALF, HALF) if first else pl.ds(0, HALF)
+        return pltpu.make_async_remote_copy(
+            src_ref=(k_hbm, v_hbm)[w].at[rows, cols] if first else detour_ref.at[w],
+            dst_ref=detour_ref.at[w] if first else (kn_ref, vn_ref)[w].at[rows, cols],
+            send_sem=detour_send.at[w],
+            recv_sem=detour_recv.at[w] if first else kv_recv.at[w, G - 1, 0],
+            device_id={"ctx": ctx(-1 if first else 2), "head": hd}, device_id_type=MESH,
+        )
+
     def relay_copy(w, g, slot, to):
         cols = pl.ds(g * HD, HD)
         near = (kn_ref, vn_ref)[w]
@@ -125,13 +138,20 @@
             device_id={"ctx": ctx(-1), "head": hd}, device_id_type=MESH,
         )
 
-    send_a = [[kv_copy(w, g, 0, 0, 1) for w in range(2)] for g in range(G)]
-    send_b = [[kv_copy(w, g, 1, 0, 2) for w in range(2)] for g in range(G)]
-    send_far = [[kv_copy(w, g, 2, HALF, 2) for w in range(2)] for g in range(G)]
-    relay_low = [[relay_copy(w, g, 1, 0) for w in range(2)] for g in range(G)]
-    relay_high = [[relay_copy(w, g, 2, 3) for w in range(2)] for g in range(G)]
+    send_a = [[kv_copy(w, g, 1, 0, 1) for w in range(2)] for g in range(G)]
+    send_b = [[kv_copy(w, g, 2, 0, 2) for w in range(2)] for g in range(G)]
+    send_far = [[kv_copy(w, g, 3, HALF, 2) for w in range(2)] for g in range(G)]
+    relay_low = [[relay_copy(w, g, 2, 1) for w in range(2)] for g in range(G)]
+    relay_high = [[relay_copy(w, g, 3, 0) for w in range(2)] for g in range(G)]
+    detour = [[detour_copy(w, first) for w in range(2)] for first in (True, False)]
 
     def send_blocks():
+
+        @pl.when(c == N_CTX - 1)
+        def _():
+            for copy in detour[0]:
+                copy.start()
+
         for g in range(G):
             for copy in send_b[g]:
                 copy.start()
@@ -146,33 +166,20 @@
                 for copy in send_far[g]:
                     copy.start()
 
+    def pass_on(received, relayed):
+        for w in range(2):
+            received[w].wait_recv()
+            relayed[w].start()
+
+    def wait_all(*groups):
+        for group in groups:
+            for copy in group:
+                copy.wait_recv()
+
     def relay(g):
-        @pl.when(odd)
+        @pl.when((y == 1) & (c != 1))
         def _():
-            for w in range(2):
-                send_b[g][w].wait_recv()
-                relay_low[g][w].start()
-
-        @pl.when(c == 1)
-        def _():
-            for w in range(2):
-                send_far[g][w].wait_recv()
-                relay_high[g][w].start()
-
-    def wait_blocks(g):
-        @pl.when(even)
-        def _():
-            for copy in send_b[g]:
-                copy.wait_recv()
-
-        for copy in send_a[g]:
-            copy.wait_recv()
-
-        @pl.when(c == 0)
-        def _():
-            for w in range(2):
-                send_far[g][w].wait_recv()
-                relay_high[g][w].wait_recv()
+            pass_on(send_b[g], relay_low[g])
 
     def compact():
         for load in loads[:5]:
@@ -220,13 +227,8 @@
         lax.fori_loop(0, 8, body, 0)
 
     def send_cache():
-        send_layer(0)
         for i in range(8):
-            there = lax.rem(z + i, 8)
-
-            @pl.when(there != 0)
-            def _():
-                send_layer(there)
+            send_layer(lax.rem(z + i, 8))
 
         cache_ref[c] = outgoing[c]
 
@@ -267,103 +269,172 @@
         lax.fori_loop(0, QPK // 4, own_heads, 0)
 
     compact()
+
+    @pl.when(z == 0)
+    def _():
+        for g in range(G):
+            own_attention(g)
+
     pl.semaphore_wait(barrier, greeted)
     send_blocks()
-    send_cache()
-    own_attention(0)
+
+    @pl.when(c != N_CTX - 2)
+    def _():
+        send_cache()
+
+    @pl.when(z != 0)
+    def _():
+        own_attention(0)
+
+    @pl.when(c == N_CTX - 2)
+    def _():
+        pass_on(*detour)
+        send_cache()
+
     relay(0)
-    own_attention(1)
-
-    @pl.when(c != 1)
-    def _():
-        relay(1)
-
-    def near_part(g, h, rs, live, acc):
-        n = (live + 127) // 128 * 128
-        qs = pl.multiple_of(h * HD, HD)
+
+    @pl.when(z != 0)
+    def _():
+        own_attention(1)
+
+    relay(1)
+
+    def weights(g, h, rs, start, n, before, unused=0):
+        keys = kn_ref[start : start + n, g * HD : (g + 1) * HD]
+        s = dot_t(q_ref[rs, pl.ds(pl.multiple_of(h * HD, HD), HD)], keys)
+        if unused:
+            s = jnp.where(iota(s.shape, 1) >= unused, s, -jnp.inf)
+        return s, jnp.maximum(before[h, rs], jnp.max(s, 1, keepdims=True))
+
+    def products(g, s, m, start, n):
+        w = jnp.exp2((s - m[:, :1]) * LOG2E_SCALE).astype(BF)
+        return w, dot(w, with_ones(vn_ref[start : start + n, g * HD : (g + 1) * HD]))
+
+    def add(acc, i, s):
+        if s.shape[1] < TOK:
+            s = jnp.concatenate([s, jnp.zeros((8, TOK - s.shape[1]), F32)], 1)
+        acc[i] = acc[i] + s
+
+    def middle_part(g, h, rs, start, n, acc, unused=0):
         st = {}
+
+        def first():
+            st["s"], st["m"] = weights(g, h, rs, start, n, m1, unused)
+
+        def second():
+            w, st["ot"] = products(g, st["s"], st["m"], start, n)
+            wm[h, rs, :n] = w
+
+        def third():
+            a = jnp.exp2((m1[h, rs] - st["m"]) * LOG2E_SCALE)
+            ot1[h, rs] = jnp.concatenate([a, a], 1) * ot1[h, rs] + st["ot"]
+            m2[h, rs] = st["m"]
+
+        return [first, second, third]
+
+    def last_part(g, h, rs, start, n, acc, middle=0):
+        st = {}
+        before = m2 if middle else m1
 
         def first():
             if n:
-                s = dot_t(q_ref[rs, pl.ds(qs, HD)], kn_ref[:n, g * HD : (g + 1) * HD])
-                if live < n:
-                    s = jnp.where(iota(s.shape, 1) < live, s, -jnp.inf)
-                st["s"] = s
-                st["m"] = jnp.maximum(m1[h, rs], jnp.max(st["s"], 1, keepdims=True))
+                st["s"], st["m"] = weights(g, h, rs, start, n, before)
 
         def second():
             if n:
-                w = jnp.exp2((st["s"] - st["m"][:, :1]) * LOG2E_SCALE).astype(BF)
-                st["w"] = w
-                st["ot"] = dot(w, with_ones(vn_ref[:n, g * HD : (g + 1) * HD]))
+                st["w"], st["ot"] = products(g, st["s"], st["m"], start, n)
 
         def third():
             o1 = ot1[h, rs]
             if n:
-                a = jnp.exp2((m1[h, rs] - st["m"]) * LOG2E_SCALE)
+                a = jnp.exp2((before[h, rs] - st["m"]) * LOG2E_SCALE)
                 inv = 1.0 / (a * o1[:, HD:] + st["ot"][:, HD:])
                 o = (a * o1[:, :HD] + st["ot"][:, :HD]) * inv
                 f = a * inv
                 s = column_sum(st["w"], inv)
-                for i in range(0, n, TOK):
-                    part = s[:, i : min(i + TOK, n)]
-                    if part.shape[1] < TOK:
-                        part = jnp.concatenate(
-                            [part, jnp.zeros((8, TOK - part.shape[1]), F32)], 1
-                        )
-                    acc[1 + i // TOK] = acc[1 + i // TOK] + part
+                add(acc, 1, s[:, :TOK])
+                if n > TOK:
+                    add(acc, 2, s[:, TOK:])
             else:
                 f = 1.0 / o1[:, HD:]
                 o = o1[:, :HD] * f
-            out_ref[rs, pl.ds(qs, HD)] = o.astype(BF)
+            out_ref[rs, pl.ds(pl.multiple_of(h * HD, HD), HD)] = o.astype(BF)
+            if middle:
+                add(acc, 2, column_sum(wm[h, rs, :middle], f))
+                f = jnp.exp2((m1[h, rs] - m2[h, rs]) * LOG2E_SCALE) * f
             if rs.start < HALF:
-                s = column_sum(wl[h], f[:HALF])
-                acc[0] = acc[0] + jnp.concatenate([s, jnp.zeros((8, TOK - 256), F32)], 1)
+                add(acc, 0, column_sum(wl[h], f[:HALF]))
             if rs.stop > HALF:
-                acc[0] = acc[0] + column_sum(wh[h], f[HALF - rs.start :])
+                add(acc, 0, column_sum(wh[h], f[HALF - rs.start :]))
 
         return [first, second, third]
 
-    def near_attention(parts, unroll, shard_one=False):
-        zero = jnp.zeros((8, TOK), F32)
-        carry = (zero, zero, zero)
+    def near_heads(g, parts, carry):
+        def heads(i, carry):
+            acc = list(carry)
+            units = []
+            for u in range(UNROLL):
+                for part, args in parts:
+                    units.append(part(g, g * QPK + i * UNROLL + u, *args[:3], acc, *args[3:]))
+            emit(units, 0)
+            return tuple(acc)
+
+        return lax.fori_loop(0, QPK // UNROLL, heads, carry)
+
+    def add_up(carry):
+        return [jnp.sum(a, 0, keepdims=True) for a in carry]
+
+    whole, low, high = slice(0, TOK), slice(0, HALF), slice(HALF, TOK)
+    left = iota((1, TOK), 1) < HALF
+    carry = (jnp.zeros((8, TOK), F32),) * 3
+
+    @pl.when(c >= 2)
+    def _():
+        acc = carry
         for g in range(G):
-            if g and shard_one:
-                relay(g)
-            wait_blocks(g)
-
-            def heads(i, carry, g=g):
-                acc = list(carry)
-                units = []
-                for u in range(unroll):
-                    for rs, n in parts:
-                        units.append(near_part(g, g * QPK + i * unroll + u, rs, n, acc))
-                emit(units, 0)
-                return tuple(acc)
-
-            carry = lax.fori_loop(0, QPK // unroll, heads, carry)
-        col_own[...] = carry[0]
-        col_near[0] = carry[1]
-        col_near[1] = carry[2]
-
-    @pl.when(c >= 2)
-    def _():
-        near_attention([(slice(0, TOK), TOK)], 8)
+
+            @pl.when(even)
+            def _():
+                wait_all(send_b[g])
+
+            wait_all(send_a[g])
+            acc = near_heads(g, [(last_part, (whole, HALF, TOK))], acc)
+        own, near, _ = add_up(acc)
+        col_send[0] = own
+        col_send[1] = jnp.where(left, near, 0.0)
+        col_send[2] = pltpu.roll(jnp.where(left, 0.0, near), HALF, 1)
 
     @pl.when(c == 1)
     def _():
-        near_attention([(slice(0, HALF), HALF), (slice(HALF, TOK), 3 * HALF)], 8, True)
+        acc = carry
+        middle = [(middle_part, (whole, 2 * HALF - 256, 256, 256 - HALF))]
+        last = [(last_part, (low, 0, 0, 256)), (last_part, (high, 2 * HALF, TOK, 256))]
+        pass_on(send_b[0], relay_low[0])
+        wait_all(send_a[0])
+        acc = near_heads(0, middle, acc)
+        pass_on(send_far[0], relay_high[0])
+        wait_all(send_a[1])
+        acc = near_heads(1, middle, acc)
+        pass_on(send_b[1], relay_low[1])
+        acc = near_heads(0, last, acc)
+        wait_all(send_far[1])
+        acc = near_heads(1, last, acc)
+        col_send[0], col_send[2], near = add_up(acc)
+        col_send[1] = pltpu.roll(near, TOK - (256 - HALF), 1)
 
     @pl.when(c == 0)
     def _():
-        near_attention([(slice(0, HALF), 0), (slice(HALF, TOK), 4 * HALF)], 8)
-
-    first = jnp.sum(col_near[0], 0, keepdims=True)
-    second = jnp.sum(col_near[1], 0, keepdims=True)
-    low = iota((1, TOK), 1) < HALF
-    col_send[0] = jnp.sum(col_own[...], 0, keepdims=True)
-    col_send[1] = jnp.where(low, first, second)
-    col_send[2] = pltpu.roll(jnp.where(low, second, first), HALF, 1)
+        acc = carry
+        parts = [(last_part, (low, 0, 0)), (last_part, (high, 0, 2 * TOK))]
+        for g in range(G):
+            wait_all(send_b[g], send_far[g], send_a[g], relay_high[g])
+            acc = near_heads(g, parts, acc)
+        own, first, second = add_up(acc)
+        first = pltpu.roll(first, HALF, 1)
+        col_send[0] = own
+        col_send[1] = first
+        col_send[2] = second
+
     sends = []
     for delta in range(3):
         for i in range(4):
@@ -408,10 +479,20 @@
             for copy in send_far[g]:
                 copy.wait_send()
 
-        @pl.when(c == 1)
-        def _():
-            for copy in relay_high[g]:
-                copy.wait_send()
+    @pl.when(c == 1)
+    def _():
+        for copy in relay_high[0]:
+            copy.wait_send()
+
+    @pl.when(c == N_CTX - 1)
+    def _():
+        for copy in detour[0]:
+            copy.wait_send()
+
+    @pl.when(c == N_CTX - 2)
+    def _():
+        for copy in detour[1]:
+            copy.wait_send()
 
 
 def tail(a_in, s_in, c_in, a_out, s_out, c_out, sem):
@@ -449,18 +530,19 @@
             pltpu.VMEM((1, G, N_CTX), jnp.int32),
             pltpu.VMEM((4 * HALF, G * HD), BF),
             pltpu.VMEM((4 * HALF, G * HD), BF),
+            pltpu.VMEM((2, HALF, HD), BF),
             pltpu.VMEM((N_CTX * 16, HD), F32),
             pltpu.VMEM((N_CTX, 16, HD), BF),
             pltpu.VMEM((HEADS, TOK, 2 * HD), F32),
             pltpu.VMEM((HEADS, TOK, HD), F32),
+            pltpu.VMEM((HEADS, TOK, HD), F32),
             pltpu.VMEM((HEADS, HALF, 256), BF),
             pltpu.VMEM((HEADS, HALF, TOK), BF),
-            pltpu.VMEM((8, TOK), F32),
-            pltpu.VMEM((2, 8, TOK), F32),
+            pltpu.VMEM((HEADS, TOK, 256), BF),
             pltpu.VMEM((3, 1, TOK), F32),
             pltpu.VMEM((12, 1, TOK), F32),
             dma((7,)), dma, dma,
-            dma((2, G, 4)), dma((2, G, 4)), dma((2, G, 4)),
+            dma((2, G, 4)), dma((2, G, 4)), dma((2, G, 4)), dma((2,)), dma((2,)),
             dma((12,)), dma((12,)),
         ],
         compiler_params=pltpu.CompilerParams(

time: 45.1 us -> 39.5 us (0.88)
  Pallas kernels: 44.2 us -> 38.6 us
    pallas_call x1, Pallas kernels: 43 us -> 37.4 us  [on_device(): pl.pallas_call(lambda *refs: kernel(*refs), name='window', out_shape=[jax...]
where the time goes in v3:
time: 39.5 us; the launch traced here: 39.4 us
  Pallas kernels  38.6 us (98%)
  between operations  0.82 us (2%)
    pallas_call x1, Pallas kernels, on_device(): pl.pallas_call(lambda *refs: kernel(*refs), name='window', out_shape=[jax...  37.4 us
    pallas_call x1, Pallas kernels, on_device(): pl.pallas_call(tail, name='tail', out_shape=[jax.ShapeDtypeStruct((TOK, H...  1.25 us

profile of v3, /device:TPU:1, one launch (start us, length us, event | category | flops | bytes accessed | tf_op | source)
XLA Modules:
  0.0 39.4 jit_solution(9655624347127444960)
XLA Ops:
  0.6 37.4 %window.1 = (bf16[384,2048]{1,0:T(8,128)(2,1)S(1)}, f32[1,384]{1,0:T(1,128)S(1)}, bf16[64,16,128]{2,1,0:T(8,128)(2,1)S(1)}) custom-call(bf16[384,2048]{1,0:T(8,128)(2,1)} %refs_0_.1, bf16[384,256]{1,0:T(8,128)(2,1)} %refs_1_.1, bf16[384,256]{1,0:T(8,128)(2,1)} %refs_2_.1, s32[1,2,4,64]{3,2,1,0:T(4,128)} %bitcast.7, s32[1,2,64]{2,1,0:T(2,128)} %refs_4_.1, ...), custom_call_target="tpu_custom_call" | custom-call | flops 2200000000 | bytes 4000000 | tf_op jit(solution)/shard_map/window/pallas_call | solution.py:514
  38.0 1.3 %tail.1 = (bf16[384,2048]{1,0:T(8,128)(2,1)}, f32[384]{0:T(512)}, bf16[64,16,128]{2,1,0:T(8,128)(2,1)}) custom-call(bf16[384,2048]{1,0:T(8,128)(2,1)S(1)} %get-tuple-element.9.a_in, f32[1,384]{1,0:T(1,128)S(1)} %get-tuple-element.10.s_in, bf16[64,16,128]{2,1,0:T(8,128)(2,1)S(1)} %get-tuple-element.11.c_in), custom_call_target="tpu_custom_call" | custom-call | tf_op jit(solution)/shard_map/tail/pallas_call | solution.py:555

commit v4 on v3

--- a/solution.py
+++ b/solution.py
@@ -57,7 +57,7 @@
     q_ref, k_ref, v_ref, rows_ref, dest_ref, count_ref,
     kn_ref, vn_ref, detour_ref, stage, outgoing,
     ot1, m1, m2, wl, wh, wm, col_send, col_recv,
-    in_sem, cache_send, cache_recv, kv_send, kv_recv, relay_send, detour_send, detour_recv,
+    in_sem, cache_send, cache_recv, kv_send, kv_recv, relay_send, detour_send, detour_recv, forward_send,
     ks_send, ks_recv,
 ):
     c = lax.axis_index("ctx")
@@ -117,15 +117,27 @@
             device_id={"ctx": ctx(delta), "head": hd}, device_id_type=MESH,
         )
 
-    def detour_copy(w, first):
-        cols = pl.ds((G - 1) * HD, HD)
-        rows = pl.ds(HALF, HALF) if first else pl.ds(0, HALF)
+    detours = [(0, 0), (1, 0), (1, 3), (0, 3), (1, 3)]
+    cols_last = pl.ds((G - 1) * HD, HD)
+
+    def detour_copy(i):
+        w, slot = detours[i]
+        step = i % 3
         return pltpu.make_async_remote_copy(
-            src_ref=(k_hbm, v_hbm)[w].at[rows, cols] if first else detour_ref.at[w],
-            dst_ref=detour_ref.at[w] if first else (kn_ref, vn_ref)[w].at[rows, cols],
-            send_sem=detour_send.at[w],
-            recv_sem=detour_recv.at[w] if first else kv_recv.at[w, G - 1, 0],
-            device_id={"ctx": ctx(-1 if first else 2), "head": hd}, device_id_type=MESH,
+            src_ref=(k_hbm, v_hbm)[w].at[pl.ds(HALF, HALF), cols_last],
+            dst_ref=detour_ref.at[step],
+            send_sem=detour_send.at[i], recv_sem=detour_recv.at[step],
+            device_id={"ctx": ctx(15 if i < 2 else 16), "head": hd}, device_id_type=MESH,
+        )
+
+    def forward_copy(i):
+        w, slot = detours[i]
+        step = i % 3
+        return pltpu.make_async_remote_copy(
+            src_ref=detour_ref.at[step],
+            dst_ref=(kn_ref, vn_ref)[w].at[pl.ds(slot * HALF, HALF), cols_last],
+            send_sem=forward_send.at[step], recv_sem=kv_recv.at[w, G - 1, slot],
+            device_id={"ctx": ctx(-14), "head": hd}, device_id_type=MESH,
         )
 
     def relay_copy(w, g, slot, to):
@@ -143,14 +155,19 @@
     send_far = [[kv_copy(w, g, 3, HALF, 2) for w in range(2)] for g in range(G)]
     relay_low = [[relay_copy(w, g, 2, 1) for w in range(2)] for g in range(G)]
     relay_high = [[relay_copy(w, g, 3, 0) for w in range(2)] for g in range(G)]
-    detour = [[detour_copy(w, first) for w in range(2)] for first in (True, False)]
+    detour = [detour_copy(i) for i in range(5)]
+    forward = [forward_copy(i) for i in range(5)]
 
     def send_blocks():
 
         @pl.when(c == N_CTX - 1)
         def _():
-            for copy in detour[0]:
-                copy.start()
+            for i in (0, 1, 3, 4):
+                detour[i].start()
+
+        @pl.when(c == N_CTX - 2)
+        def _():
+            detour[2].start()
 
         for g in range(G):
             for copy in send_b[g]:
@@ -161,10 +178,16 @@
                 for copy in send_a[g]:
                     copy.start()
 
-            @pl.when(c >= N_CTX - 2)
-            def _():
-                for copy in send_far[g]:
-                    copy.start()
+            if g == 0:
+
+                @pl.when(c >= N_CTX - 2)
+                def _():
+                    for copy in send_far[0]:
+                        copy.start()
+
+        @pl.when(c == N_CTX - 2)
+        def _():
+            send_far[1][0].start()
 
     def pass_on(received, relayed):
         for w in range(2):
@@ -278,7 +301,9 @@
     pl.semaphore_wait(barrier, greeted)
     send_blocks()
 
-    @pl.when(c != N_CTX - 2)
+    by_way = (c == 14) | (c == 15)
+
+    @pl.when(jnp.logical_not(by_way))
     def _():
         send_cache()
 
@@ -286,9 +311,20 @@
     def _():
         own_attention(0)
 
-    @pl.when(c == N_CTX - 2)
-    def _():
-        pass_on(*detour)
+    @pl.when(by_way)
+    def _():
+        @pl.when(c == 14)
+        def _():
+            for i in (2, 0, 1):
+                detour[i].wait_recv()
+                forward[i].start()
+
+        @pl.when(c == 15)
+        def _():
+            for i in (3, 4):
+                detour[i].wait_recv()
+                forward[i].start()
+
         send_cache()
 
     relay(0)
@@ -332,13 +368,13 @@
 
         return [first, second, third]
 
-    def last_part(g, h, rs, start, n, acc, middle=0):
+    def last_part(g, h, rs, start, n, acc, middle=0, unused=0, to=1):
         st = {}
         before = m2 if middle else m1
 
         def first():
             if n:
-                st["s"], st["m"] = weights(g, h, rs, start, n, before)
+                st["s"], st["m"] = weights(g, h, rs, start, n, before, unused)
 
         def second():
             if n:
@@ -352,7 +388,7 @@
                 o = (a * o1[:, :HD] + st["ot"][:, :HD]) * inv
                 f = a * inv
                 s = column_sum(st["w"], inv)
-                add(acc, 1, s[:, :TOK])
+                add(acc, to, s[:, :TOK])
                 if n > TOK:
                     add(acc, 2, s[:, TOK:])
             else:
@@ -407,8 +443,12 @@
     @pl.when(c == 1)
     def _():
         acc = carry
-        middle = [(middle_part, (whole, 2 * HALF - 256, 256, 256 - HALF))]
-        last = [(last_part, (low, 0, 0, 256)), (last_part, (high, 2 * HALF, TOK, 256))]
+        start, unused = 2 * HALF - 256, 256 - HALF
+        middle = [
+            (last_part, (low, start, 256, 0, unused, 2)),
+            (middle_part, (high, start, 256, unused)),
+        ]
+        last = [(last_part, (high, 2 * HALF, TOK, 256))]
         pass_on(send_b[0], relay_low[0])
         wait_all(send_a[0])
         acc = near_heads(0, middle, acc)
@@ -425,10 +465,11 @@
     @pl.when(c == 0)
     def _():
         acc = carry
-        parts = [(last_part, (low, 0, 0)), (last_part, (high, 0, 2 * TOK))]
+        for g in range(G):
+            acc = near_heads(g, [(last_part, (low, 0, 0))], acc)
         for g in range(G):
             wait_all(send_b[g], send_far[g], send_a[g], relay_high[g])
-            acc = near_heads(g, parts, acc)
+            acc = near_heads(g, [(last_part, (high, 0, 2 * TOK))], acc)
         own, first, second = add_up(acc)
         first = pltpu.roll(first, HALF, 1)
         col_send[0] = own
@@ -474,24 +515,34 @@
             for copy in relay_low[g]:
                 copy.wait_send()
 
-        @pl.when(c >= N_CTX - 2)
-        def _():
-            for copy in send_far[g]:
-                copy.wait_send()
+    @pl.when(c >= N_CTX - 2)
+    def _():
+        for copy in send_far[0]:
+            copy.wait_send()
+
+    @pl.when(c == N_CTX - 2)
+    def _():
+        send_far[1][0].wait_send()
+        detour[2].wait_send()
+
+    @pl.when(c == N_CTX - 1)
+    def _():
+        for i in (0, 1, 3, 4):
+            detour[i].wait_send()
+
+    @pl.when(c == 14)
+    def _():
+        for i in (0, 1, 2):
+            forward[i].wait_send()
+
+    @pl.when(c == 15)
+    def _():
+        for i in (3, 4):
+            forward[i].wait_send()
 
     @pl.when(c == 1)
     def _():
         for copy in relay_high[0]:
-            copy.wait_send()
-
-    @pl.when(c == N_CTX - 1)
-    def _():
-        for copy in detour[0]:
-            copy.wait_send()
-
-    @pl.when(c == N_CTX - 2)
-    def _():
-        for copy in detour[1]:
             copy.wait_send()
 
 
@@ -530,7 +581,7 @@
             pltpu.VMEM((1, G, N_CTX), jnp.int32),
             pltpu.VMEM((4 * HALF, G * HD), BF),
             pltpu.VMEM((4 * HALF, G * HD), BF),
-            pltpu.VMEM((2, HALF, HD), BF),
+            pltpu.VMEM((3, HALF, HD), BF),
             pltpu.VMEM((N_CTX * 16, HD), F32),
             pltpu.VMEM((N_CTX, 16, HD), BF),
             pltpu.VMEM((HEADS, TOK, 2 * HD), F32),
@@ -542,7 +593,7 @@
             pltpu.VMEM((3, 1, TOK), F32),
             pltpu.VMEM((12, 1, TOK), F32),
             dma((7,)), dma, dma,
-            dma((2, G, 4)), dma((2, G, 4)), dma((2, G, 4)), dma((2,)), dma((2,)),
+            dma((2, G, 4)), dma((2, G, 4)), dma((2, G, 4)), dma((5,)), dma((3,)), dma((3,)),
             dma((12,)), dma((12,)),
         ],
         compiler_params=pltpu.CompilerParams(

time: 39.5 us -> 38.8 us (0.982)
  Pallas kernels: 38.6 us -> 37.9 us
    pallas_call x1, Pallas kernels: 37.4 us -> 36.6 us  [on_device(): pl.pallas_call(lambda *refs: kernel(*refs), name='window', out_shape=[jax...]
where the time goes in v4:
time: 38.8 us; the launch traced here: 38.7 us
  Pallas kernels  37.9 us (98%)
  between operations  0.82 us (2%)
    pallas_call x1, Pallas kernels, on_device(): pl.pallas_call(lambda *refs: kernel(*refs), name='window', out_shape=[jax...  36.6 us
    pallas_call x1, Pallas kernels, on_device(): pl.pallas_call(tail, name='tail', out_shape=[jax.ShapeDtypeStruct((TOK, H...  1.25 us

profile of v4, /device:TPU:1, one launch (start us, length us, event | category | flops | bytes accessed | tf_op | source)
XLA Modules:
  0.0 38.7 jit_solution(3810958402908345089)
XLA Ops:
  0.6 36.6 %window.1 = (bf16[384,2048]{1,0:T(8,128)(2,1)S(1)}, f32[1,384]{1,0:T(1,128)S(1)}, bf16[64,16,128]{2,1,0:T(8,128)(2,1)S(1)}) custom-call(bf16[384,2048]{1,0:T(8,128)(2,1)} %refs_0_.1, bf16[384,256]{1,0:T(8,128)(2,1)} %refs_1_.1, bf16[384,256]{1,0:T(8,128)(2,1)} %refs_2_.1, s32[1,2,4,64]{3,2,1,0:T(4,128)} %bitcast.7, s32[1,2,64]{2,1,0:T(2,128)} %refs_4_.1, ...), custom_call_target="tpu_custom_call" | custom-call | flops 2200000000 | bytes 4000000 | tf_op jit(solution)/shard_map/window/pallas_call | solution.py:565
  37.3 1.3 %tail.1 = (bf16[384,2048]{1,0:T(8,128)(2,1)}, f32[384]{0:T(512)}, bf16[64,16,128]{2,1,0:T(8,128)(2,1)}) custom-call(bf16[384,2048]{1,0:T(8,128)(2,1)S(1)} %get-tuple-element.9.a_in, f32[1,384]{1,0:T(1,128)S(1)} %get-tuple-element.10.s_in, bf16[64,16,128]{2,1,0:T(8,128)(2,1)S(1)} %get-tuple-element.11.c_in), custom_call_target="tpu_custom_call" | custom-call | tf_op jit(solution)/shard_map/tail/pallas_call | solution.py:606

commit v5 on v4

--- a/solution.py
+++ b/solution.py
@@ -477,7 +477,7 @@
         col_send[2] = second
 
     sends = []
-    for delta in range(3):
+    for delta in (2, 1, 0):
         for i in range(4):
             if delta or i:
                 sends.append(
@@ -548,10 +548,12 @@
 
 def tail(a_in, s_in, c_in, a_out, s_out, c_out, sem):
     copies = [
-        pltpu.make_async_copy(a_in, a_out, sem.at[0]),
+        pltpu.make_async_copy(s_in.at[0], s_out, sem.at[0]),
         pltpu.make_async_copy(c_in, c_out, sem.at[1]),
-        pltpu.make_async_copy(s_in.at[0], s_out, sem.at[2]),
     ]
+    for i in range(4):
+        rows = pl.ds(i * (TOK // 4), TOK // 4)
+        copies.append(pltpu.make_async_copy(a_in.at[rows], a_out.at[rows], sem.at[2 + i]))
     for copy in copies:
         copy.start()
     for copy in copies:
@@ -613,7 +615,7 @@
         ],
         in_specs=[anywhere] * 3,
         out_specs=[anywhere] * 3,
-        scratch_shapes=[dma((3,))],
+        scratch_shapes=[dma((6,))],
         compiler_params=pltpu.CompilerParams(vmem_limit_bytes=1 << 20),
     )(*results)
     cache = cache.reshape(N_CTX, KB, 2, G, HD).transpose(0, 1, 3, 2, 4)

time: 38.8 us -> 38.9 us (level)
  no operation moved by 1% of the time
where the time goes in v5:
time: 38.9 us; the launch traced here: 38.8 us
  Pallas kernels  37.9 us (97%)
  between operations  0.82 us (2%)
    pallas_call x1, Pallas kernels, on_device(): pl.pallas_call(lambda *refs: kernel(*refs), name='window', out_shape=[jax...  36.7 us
    pallas_call x1, Pallas kernels, on_device(): pl.pallas_call(tail, name='tail', out_shape=[jax.ShapeDtypeStruct((TOK, H...  1.28 us

profile of v5, /device:TPU:1, one launch (start us, length us, event | category | flops | bytes accessed | tf_op | source)
XLA Modules:
  0.0 38.8 jit_solution(1988418135883567199)
XLA Ops:
  0.6 36.7 %window.1 = (bf16[384,2048]{1,0:T(8,128)(2,1)S(1)}, f32[1,384]{1,0:T(1,128)S(1)}, bf16[64,16,128]{2,1,0:T(8,128)(2,1)S(1)}) custom-call(bf16[384,2048]{1,0:T(8,128)(2,1)} %refs_0_.1, bf16[384,256]{1,0:T(8,128)(2,1)} %refs_1_.1, bf16[384,256]{1,0:T(8,128)(2,1)} %refs_2_.1, s32[1,2,4,64]{3,2,1,0:T(4,128)} %bitcast.7, s32[1,2,64]{2,1,0:T(2,128)} %refs_4_.1, ...), custom_call_target="tpu_custom_call" | custom-call | flops 2200000000 | bytes 4000000 | tf_op jit(solution)/shard_map/window/pallas_call | solution.py:567
  37.3 1.3 %tail.1 = (bf16[384,2048]{1,0:T(8,128)(2,1)}, f32[384]{0:T(512)}, bf16[64,16,128]{2,1,0:T(8,128)(2,1)}) custom-call(bf16[384,2048]{1,0:T(8,128)(2,1)S(1)} %get-tuple-element.9.a_in, f32[1,384]{1,0:T(1,128)S(1)} %get-tuple-element.10.s_in, bf16[64,16,128]{2,1,0:T(8,128)(2,1)S(1)} %get-tuple-element.11.c_in), custom_call_target="tpu_custom_call" | custom-call | tf_op jit(solution)/shard_map/tail/pallas_call | solution.py:608
